TPU v7x, 128 devices: a whole 4x4x4 slice. The times are simulated.
128 devices in a mesh: ctx: 16 (over z, y_hi, core), exp: 8 (over x, y_lo).
Axes of the slice: x: 4, y: 4 (y_hi: 2, y_lo: 2; y = y_hi * 2 + y_lo), z: 4, core: 2. Of those that a mesh axis runs over, the one named last changes fastest.
Arguments:
- tokens: bfloat16 [16384, 2048], P(('ctx', 'exp')), may hold values from -12 to 12
- ln1_gain: float32 [2048], replicated, may hold values from 0.5 to 2
- w_query: bfloat16 [2048, 2048], P(None, 'exp')
- key_weight: bfloat16 [2048, 256], replicated
- value_weight: bfloat16 [2048, 256], replicated, may hold values from -0.125 to 0.125
- q_gain: float32 [128], replicated, may hold values from 0.5 to 5.5
- k_gain: float32 [128], replicated, may hold values from 0.5 to 5.5
- w_out: bfloat16 [2048, 2048], P('exp'), may hold values from -0.125 to 0.125
- ln2_gain: float32 [2048], replicated, may hold values from 0.5 to 2
- expert_ids: int32 [16384, 8], P(('ctx', 'exp')), may hold values from 0 to 127, all different within a row; in each aligned block of 128 rows (0 to 127, 128 to 255, ...) at most 12 rows name the same one
- route_weights: int32 [16384, 8], P(('ctx', 'exp')), may hold values from 1 to 255
- w_gate: bfloat16 [128, 2048, 768], P(('ctx', 'exp')), may hold values from -0.125 to 0.125
- w_up: bfloat16 [128, 2048, 768], P(('ctx', 'exp')), may hold values from -0.125 to 0.125
- w_down: bfloat16 [128, 768, 2048], P(('ctx', 'exp')), may hold values from -0.21875 to 0.21875
Outputs:
- layer_out: bfloat16 [16384, 2048], P(('ctx', 'exp'))
Inputs may be any that keep to these rules, and one draw needn't show every extreme that they name: `expert_ids`: each token names 8 different experts; among the 128 rows of one device no expert is named by more than 12 rows. `route_weights`: a choice weighs the value divided by 1024.
All inputs are finite; a program needn't handle non-finite values.
Results may differ from a plain program's by a relative error of at most 0.02.
The roundings to bfloat16 on the way count: a program that leaves them out, or rounds other values in their place, can miss the bound.
Values may be sent and summed in bfloat16 or wider, within the bound.
A program may use at most 128 MiB of HBM per device.

v0:
```python
import jax
import jax.numpy as jnp
from jax import lax
from jax.sharding import PartitionSpec as P

HEAD_SIZE = 128
QUERY_HEADS = 16
KEY_VALUE_HEADS = 2
TOP = 8


eps_value = 1e-06
theta_value = 1000000.0
floor_value = -1e30
block_span = 1024


def rms_scale(value_states, norm_gain):
    return (
        value_states
        * lax.rsqrt(jnp.mean(value_states * value_states, axis=-1, keepdims=True) + eps_value)
        * norm_gain
    )


def rotate(value_states, positions):
    half_size = value_states.shape[-1] // 2
    frequency = theta_value ** (
        -2.0 * jnp.arange(half_size, dtype=jnp.float32) / value_states.shape[-1]
    )
    angles = positions.astype(jnp.float32)[:, None] * frequency[None, :]
    cosine = jnp.cos(angles)
    sine_part = jnp.sin(angles)
    leading = value_states[..., :half_size]
    second = value_states[..., half_size:]
    return jnp.concatenate(
        [leading * cosine - second * sine_part, second * cosine + leading * sine_part], axis=-1
    )


def attend_block(carried, group_queries, group_first, key_rows, value_rows, key_first):
    running_max, running_sum, weighted = carried
    scores = jnp.einsum(
        "hqd,kd->hqk", group_queries, key_rows, preferred_element_type=jnp.float32
    ) * group_queries.shape[-1] ** (-0.5)
    query_pos = group_first + jnp.arange(group_queries.shape[1])
    key_pos = key_first + jnp.arange(key_rows.shape[0])
    visible = key_pos[None, :] <= query_pos[:, None]
    scores = jnp.where(visible[None], scores, -jnp.inf)
    new_max = jnp.maximum(running_max, jnp.max(scores, axis=-1))
    weights = jnp.exp(scores - new_max[..., None])
    rescale = jnp.exp(running_max - new_max)
    running_sum = running_sum * rescale + jnp.sum(weights, axis=-1)
    weighted = weighted * rescale[..., None] + jnp.einsum(
        "hqk,kd->hqd", weights.astype(jnp.bfloat16), value_rows, preferred_element_type=jnp.float32
    )
    return (new_max, running_sum, weighted)


def scan_keys(group_state, group_queries, group_first, key_rows, value_rows, step_rows):
    group_last = group_first + group_queries.shape[1] - 1

    def one_block(block_index, carried):
        key_first = block_index * step_rows
        key_part = lax.dynamic_slice_in_dim(key_rows, block_index * step_rows, step_rows, 0)
        value_part = lax.dynamic_slice_in_dim(value_rows, block_index * step_rows, step_rows, 0)
        return lax.cond(
            key_first > group_last,
            lambda current: current,
            lambda current: attend_block(
                current, group_queries, group_first, key_part, value_part, key_first
            ),
            carried,
        )

    return lax.fori_loop(0, key_rows.shape[0] // step_rows, one_block, group_state)


def shards(
    tokens,
    ln1_gain,
    w_query,
    key_weight,
    value_weight,
    q_gain,
    k_gain,
    w_out,
    ln2_gain,
    expert_ids,
    route_weights,
    w_gate,
    w_up,
    w_down,
):
    rows_dev = tokens.shape[0]
    ctx_count = lax.axis_size("ctx")
    exp_count = lax.axis_size("exp")
    ctx_rows = rows_dev * exp_count
    heads_dev = w_query.shape[1] // HEAD_SIZE
    group_width = QUERY_HEADS // KEY_VALUE_HEADS
    kv_head = lax.axis_index("exp") * heads_dev // group_width
    inputs32 = tokens.astype(jnp.float32)
    normed_input = rms_scale(inputs32, ln1_gain).astype(jnp.bfloat16)
    key_cols = lax.dynamic_slice_in_dim(key_weight, kv_head * HEAD_SIZE, HEAD_SIZE, 1)
    value_cols = lax.dynamic_slice_in_dim(value_weight, kv_head * HEAD_SIZE, HEAD_SIZE, 1)
    joined = jnp.concatenate([w_query, key_cols, value_cols], axis=1)
    projected = jnp.dot(
        lax.all_gather(normed_input, "exp", axis=0, tiled=True),
        joined,
        preferred_element_type=jnp.float32,
    )
    ctx_first = lax.axis_index("ctx") * ctx_rows
    positions = ctx_first + jnp.arange(ctx_rows)
    query_cols = heads_dev * HEAD_SIZE
    query_heads = (
        projected[:, :query_cols].reshape(ctx_rows, heads_dev, HEAD_SIZE).transpose(1, 0, 2)
    )
    queries = rotate(rms_scale(query_heads, q_gain), positions).astype(jnp.bfloat16)
    keys_all = rotate(
        rms_scale(projected[:, query_cols : query_cols + HEAD_SIZE], k_gain), positions
    ).astype(jnp.bfloat16)
    values_all = projected[:, query_cols + HEAD_SIZE :].astype(jnp.bfloat16)
    groups = ((queries, ctx_first),)
    initial = tuple(
        (
            (
                jnp.full((heads_dev, group_queries.shape[1]), floor_value, jnp.float32),
                jnp.zeros((heads_dev, group_queries.shape[1]), jnp.float32),
                jnp.zeros((heads_dev, group_queries.shape[1], HEAD_SIZE), jnp.float32),
            )
            for group_queries, group_first in groups
        )
    )
    key_rows = lax.all_gather(keys_all, "ctx", axis=0, tiled=True)
    value_rows = lax.all_gather(values_all, "ctx", axis=0, tiled=True)
    finals = tuple(
        (
            scan_keys(group_state, group_queries, group_first, key_rows, value_rows, block_span)
            for (group_queries, group_first), group_state in zip(groups, initial)
        )
    )
    outputs = [
        (weighted / running_sum[..., None]).astype(jnp.bfloat16)
        for running_max, running_sum, weighted in finals
    ]
    merged = outputs[0]
    attended = merged.transpose(1, 0, 2).reshape(ctx_rows, query_cols)
    attention = lax.psum_scatter(
        jnp.dot(attended, w_out, preferred_element_type=jnp.float32).astype(jnp.bfloat16),
        "exp",
        scatter_dimension=0,
        tiled=True,
    ).astype(jnp.float32)
    residual = (inputs32 + attention).astype(jnp.bfloat16)
    normed2 = rms_scale(residual.astype(jnp.float32), ln2_gain).astype(jnp.bfloat16)
    experts = ctx_count * exp_count
    capacity = max(2, 3 * rows_dev * TOP // (2 * experts))
    chosen = expert_ids[:, :, None] == jnp.arange(experts)[None, None, :]
    counts = jnp.sum(chosen, axis=1, dtype=jnp.int32)
    rank_table = jnp.cumsum(counts, axis=0, dtype=jnp.int32) - counts
    slot_index = jnp.sum(jnp.where(chosen, rank_table[:, None, :], 0), axis=2)
    slot_hot = slot_index[:, :, None] == jnp.arange(capacity)[None, None, :]
    dispatch = jnp.einsum(
        "tke,tkc->ect",
        chosen.astype(jnp.bfloat16),
        slot_hot.astype(jnp.bfloat16),
        preferred_element_type=jnp.float32,
    ).astype(jnp.bfloat16)
    outgoing = jnp.einsum(
        "ect,td->ecd", dispatch, normed2, preferred_element_type=jnp.float32
    ).astype(jnp.bfloat16)
    weight_frac = route_weights.astype(jnp.float32) / 1024.0
    combine = jnp.einsum(
        "tke,tkc->tec",
        chosen.astype(jnp.float32) * weight_frac[:, :, None],
        slot_hot.astype(jnp.float32),
    ).astype(jnp.bfloat16)
    width = outgoing.shape[2]
    arrived = lax.all_to_all(outgoing, ("ctx", "exp"), split_axis=0, concat_axis=0, tiled=True)
    flat_rows = arrived.reshape(-1, width)
    gate_act = jnp.dot(flat_rows, w_gate[0], preferred_element_type=jnp.float32)
    up_act = jnp.dot(flat_rows, w_up[0], preferred_element_type=jnp.float32)
    hidden = (jax.nn.silu(gate_act) * up_act).astype(jnp.bfloat16)
    produced = jnp.dot(hidden, w_down[0], preferred_element_type=jnp.float32).astype(jnp.bfloat16)
    returned = lax.all_to_all(
        produced.reshape(arrived.shape), ("ctx", "exp"), split_axis=0, concat_axis=0, tiled=True
    )
    mixture = jnp.einsum("tec,ecd->td", combine, returned, preferred_element_type=jnp.float32)
    return (residual.astype(jnp.float32) + mixture).astype(jnp.bfloat16)


def solution(mesh):
    in_specs = (
        P(("ctx", "exp"), None),
        P(),
        P(None, "exp"),
        P(),
        P(),
        P(),
        P(),
        P("exp", None),
        P(),
        P(("ctx", "exp"), None),
        P(("ctx", "exp"), None),
        P(("ctx", "exp"), None, None),
        P(("ctx", "exp"), None, None),
        P(("ctx", "exp"), None, None),
    )
    out_specs = P(("ctx", "exp"), None)
    return jax.shard_map(shards, mesh=mesh, in_specs=in_specs, out_specs=out_specs, check_vma=False)
```

profile of v0, /device:TPU:1, one launch (start us, length us, event | category | flops | bytes accessed | tf_op | source)
XLA Modules:
  0.0 801.3 jit_solution(13334901165268081912)
XLA Ops:
  6.5 1.4 fusion.40
  7.9 2.0 fusion.42
  10.1 2.2 constant_dynamic-slice_fusion
  12.3 90.7 %all-gather.4.cloned.1.call-done = bf16[1024,2048]{1,0:T(8,128)(2,1)} async-done(((bf16[128,2048]{1,0:T(8,128)(2,1)}), bf16[1024,2048]{1,0:T(8,128)(2,1)}) %all-gather.4.cloned.1.call-update) | async-done | bytes 4194320 | tf_op jit(solution)/shard_map/all_gather | solution.py:108
  103.1 5.2 fusion.33
  108.3 1.3 copy-done.5
  109.7 1.8 multiply_cosine_fusion
  112.3 1.8 slice.47
  114.2 2.3 slice.32
  116.5 2.5 copy.36
  119.1 1.9 copy.38
  122.0 1.6 fusion.47
  123.6 1.6 fusion.48
  125.2 1.7 subtract_convert_fusion
  128.1 42.8 %all-gather.6.cloned.1.call-done = bf16[16384,128]{0,1:T(8,128)(2,1)} async-done(((bf16[1024,128]{0,1:T(8,128)(2,1)}), bf16[16384,128]{0,1:T(8,128)(2,1)}) %all-gather.6.cloned.1.call-update) | async-done | bytes 4194320 | tf_op jit(solution)/shard_map/all_gather | solution.py:134
  170.9 6.9 copy.39
  177.7 48.8 %all-gather.8.cloned.1.call-done = bf16[16384,128]{0,1:T(8,128)(2,1)} async-done(((bf16[1024,128]{0,1:T(8,128)(2,1)}), bf16[16384,128]{0,1:T(8,128)(2,1)}) %all-gather.8.cloned.1.call-update) | async-done | bytes 4194320 | tf_op jit(solution)/shard_map/all_gather | solution.py:135
  226.5 6.4 copy.40
  234.1 24.2 %while.17 = (s32[]{:T(128)}, f32[2,1024]{1,0:T(2,128)S(1)}, f32[2,1024]{1,0:T(2,128)S(1)}, f32[2,1024,128]{2,1,0:T(8,128)}, s32[]{:T(128)}, /*index=5*/s32[]{:T(...) while((s32[]{:T(128)}, f32[2,1024]{1,0:T(2,128)S(1)}, ...), condition=%wide.region_8.9_spmd, body=%wide.region_3.8_spmd.sunk | while | flops 1098389504 | bytes 45236608 | solution.py:76
  234.1 11.6 %conditional.2 = (f32[2,1024]{1,0:T(2,128)S(1)}, f32[2,1024]{1,0:T(2,128)S(1)}, f32[2,1024,128]{2,1,0:T(8,128)}) conditional(s32[]{:T(128)} %convert_element_type.167, (s32[]{:T(128)}, s32[]{:T(128)}, bf16[16384,128]{1,0:T(8,128)(2,1)}, bf16[2,1024,128]{2,1,0:T(8,128)(2,1)}, f32[2,1024]{1,0:T(2,128)S(1)}, /*index=5*/f32[2,1024]{1,0:T(2,128)S(1)}, ...), branch_computations={%region_4.6_spmd, %region_7.7_spmd} | conditional | flops 1098389504 | bytes 45219996 | solution.py:67
  234.1 1.6 broadcast_compare_fusion
  235.7 3.3 fusion.2
  239.0 2.0 fusion.1
  241.0 3.6 fusion.6
  245.7 11.6 %conditional.2 = (f32[2,1024]{1,0:T(2,128)S(1)}, f32[2,1024]{1,0:T(2,128)S(1)}, f32[2,1024,128]{2,1,0:T(8,128)}) conditional(s32[]{:T(128)} %convert_element_type.167, (s32[]{:T(128)}, s32[]{:T(128)}, bf16[16384,128]{1,0:T(8,128)(2,1)}, bf16[2,1024,128]{2,1,0:T(8,128)(2,1)}, f32[2,1024]{1,0:T(2,128)S(1)}, /*index=5*/f32[2,1024]{1,0:T(2,128)S(1)}, ...), branch_computations={%region_4.6_spmd, %region_7.7_spmd} | conditional | flops 1098389504 | bytes 45219996 | solution.py:67
  245.7 1.6 broadcast_compare_fusion
  247.3 3.3 fusion.2
  250.7 2.0 fusion.1
  252.7 3.6 fusion.6
  258.3 2.5 copy.41
  260.8 1.3 divide_convert_fusion
  262.1 4.5 convolution_convert_fusion.2
  267.2 2.4 select_reduce_fusion
  269.6 2.0 fusion.39
  271.5 244.4 %reduce-scatter.2.cloned.1.call-done = bf16[128,2048]{1,0:T(8,128)(2,1)} async-done(((bf16[1024,2048]{1,0:T(8,128)(2,1)}), bf16[128,2048]{1,0:T(8,128)(2,1)}) %reduce-scatter.2.cloned.1.call-update) | async-done | bytes 524304 | tf_op jit(solution)/shard_map/reduce_scatter | solution.py:148
  515.9 1.5 fusion.44
  517.4 3.2 convolution_convert_fusion.1
  520.7 6.9 copy.45
  527.5 106.6 %all_to_all.10 = bf16[128,12,2048]{2,1,0:T(8,128)(2,1)} all-to-all(bf16[128,12,2048]{2,1,0:T(8,128)(2,1)} %copy.45), channel_id=1, replica_groups=mesh['ctx'=16,'exp'=8] {'ctx','exp'}, dimensions={0} | all-to-all | bytes 12582912 | tf_op jit(solution)/shard_map/all_to_all | solution.py:179
  634.1 10.7 %reshape.167 = bf16[1536,2048]{1,0:T(8,128)(2,1)} reshape(bf16[128,12,2048]{2,1,0:T(8,128)(2,1)} %all_to_all.10) | data formatting | bytes 12582912 | tf_op jit(solution)/shard_map/reshape | solution.py:180
  644.8 8.2 %fusion.22 = f32[1536,768]{1,0:T(8,128)S(1)} fusion(bf16[1536,2048]{1,0:T(8,128)(2,1)} %reshape.167, bf16[1,2048,768]{2,1,0:T(8,128)(2,1)} %param.29), kind=kOutput, calls=%fused_computation.30 | convolution fusion | flops 4831838208 | bytes 14155776 | tf_op jit(solution)/shard_map/dot_general | solution.py:181
  653.0 5.6 multiply_convert_fusion
  658.7 7.1 convolution_convert_fusion
  665.7 10.6 %reshape.168 = bf16[128,12,2048]{2,1,0:T(8,128)(2,1)} reshape(bf16[1536,2048]{1,0:T(8,128)(2,1)} %convolution_convert_fusion) | data formatting | bytes 12582912 | tf_op jit(solution)/shard_map/reshape | solution.py:186
  676.3 6.9 all-to-all-start.1
  683.4 2.0 convolution_convert_fusion.3
  685.4 97.5 %all-to-all-done.1 = bf16[128,12,2048]{2,1,0:T(8,128)(2,1)} async-done(((bf16[128,12,2048]{2,1,0:T(8,128)(2,1)}), bf16[128,12,2048]{2,1,0:T(8,128)(2,1)}, u32[]{:S(2)}, u32[]{:S(2)}) %all-to-all-start.1) | async-done | bytes 6291488 | tf_op jit(solution)/shard_map/all_to_all | solution.py:185
  782.9 11.6 %fusion.30 = bf16[128,2048]{1,0:T(8,128)(2,1)} fusion(bf16[128,12,2048]{2,1,0:T(8,128)(2,1)} %all-to-all-done.1, bf16[128,128,12]{1,2,0:T(8,128)(2,1)} %convolution_convert_fusion.3, bf16[128,2048]{1,0:T(8,128)(2,1)} %reduce-scatter.2.cloned.1.call-done, bf16[128,2048]{1,0:T(8,128)(2,1)} %param.18), kind=kOutput, calls=%fused_computation.34 | convolution fusion | flops 807141376 | bytes 8257536 | tf_op jit(solution)/shard_map/tec,ecd->td/dot_general | solution.py:188
  (107 shorter events, 7.6 us)
Async XLA Ops:
  6.5 652.1 %copy-start = (bf16[1,768,2048]{2,1,0:T(8,128)(2,1)S(1)}, bf16[1,768,2048]{2,1,0:T(8,128)(2,1)}, u32[]{:S(2)}) copy-start(bf16[1,768,2048]{2,1,0:T(8,128)(2,1)} %param.31) | copy-start | bytes 9437188
  6.5 96.5 %all-gather.4.cloned.1.call-start = ((), (), s32[]{:S(2)}) async-start(), calls=%async_computation.3 | async-start | bytes 4718592 | tf_op jit(solution)/shard_map/all_gather | solution.py:108
  10.0 160.9 %all-gather.6.cloned.1.call-start = ((), (), s32[]{:S(2)}) async-start(), calls=%async_computation.4 | async-start | bytes 4456448 | tf_op jit(solution)/shard_map/all_gather | solution.py:134
  103.1 6.6 copy-start.9
  108.3 1.4 copy-start.5
  109.7 13.9 %copy-start.10 = (f32[128]{0:T(128)S(1)}, f32[128]{0:T(128)}, u32[]{:S(2)}) copy-start(f32[128]{0:T(128)} %param.23) | copy-start | bytes 1540
  112.3 114.2 %all-gather.8.cloned.1.call-start = ((), (), s32[]{:S(2)}) async-start(), calls=%async_computation.5 | async-start | bytes 4456448 | tf_op jit(solution)/shard_map/all_gather | solution.py:135
  114.2 401.8 %reduce-scatter.2.cloned.1.call-start = ((), (), s32[]{:S(2)}) async-start(), calls=%async_computation.6 | async-start | bytes 4718592 | tf_op jit(solution)/shard_map/reduce_scatter | solution.py:148
  235.7 3.3 copy-start.1
  239.0 2.0 copy-start.3
  244.6 1.1 copy-start.4
  247.3 3.3 copy-start.1
  250.7 2.0 copy-start.3
  256.3 1.1 copy-start.4
  262.1 4.5 copy-start.7
  266.6 250.8 %copy-start.6 = (f32[2048]{0:T(1024)S(1)}, f32[2048]{0:T(1024)}, u32[]{:S(2)}) copy-start(f32[2048]{0:T(1024)} %param.26) | copy-start | bytes 24580
  644.8 8.2 %copy-start.2 = (bf16[1536,2048]{1,0:T(8,128)(2,1)S(1)}, bf16[1536,2048]{1,0:T(8,128)(2,1)}, u32[]{:S(2)}) copy-start(bf16[1536,2048]{1,0:T(8,128)(2,1)} %reshape.167) | copy-start | bytes 18874372
  644.8 8.2 %copy-start.11 = (bf16[1,2048,768]{2,1,0:T(8,128)(2,1)S(1)}, bf16[1,2048,768]{2,1,0:T(8,128)(2,1)}, u32[]{:S(2)}) copy-start(bf16[1,2048,768]{2,1,0:T(8,128)(2,1)} %param.30) | copy-start | bytes 9437188
  676.3 7.0 copy-start.8
  676.3 106.5 %all-to-all-start.1 = ((bf16[128,12,2048]{2,1,0:T(8,128)(2,1)}), bf16[128,12,2048]{2,1,0:T(8,128)(2,1)}, u32[]{:S(2)}, u32[]{:S(2)}) async-start(bf16[128,12,2048]{2,1,0:T(8,128)(2,1)} %reshape.168), calls=%async_computation.2 | async-start | bytes 16777216 | tf_op jit(solution)/shard_map/all_to_all | solution.py:185
Sparse Core Ops, SparseCore 0:
  10.1 92.9 all-gather.3
  112.4 58.3 all-gather.5
  173.3 53.1 all-gather.7
  266.8 249.1 reduce-scatter.1
where the time goes:
time: 811 us; the launch traced here: 801 us
  waiting for transfers between devices  524 us (65%)
  blocking collectives  107 us (13%)
  matrix products  63.1 us (8%)
  local copies, waits for them, and re-layouts  60.7 us (7%)
  other arithmetic  24.9 us (3%)
  between operations  13.7 us (2%)
    reduce_scatter x1, waiting for transfers between devices, shards(): lax.psum_scatter(jnp.dot(attended, w_out, preferred_element_type=jnp.floa...  244 us
    all_to_all x1, blocking collectives, shards(): lax.all_to_all(outgoing, ('ctx', 'exp'), split_axis=0, concat_axis=0, til...  107 us
    all_to_all x1, waiting for transfers between devices, shards(): lax.all_to_all(produced.reshape(arrived.shape), ('ctx', 'exp'), split_axi...  97.5 us
    all_gather x1, waiting for transfers between devices, shards(): lax.all_gather(normed_input, 'exp', axis=0, tiled=True)  90.7 us
    all_gather x1, waiting for transfers between devices, shards(): value_rows = lax.all_gather(values_all, 'ctx', axis=0, tiled=True)  48.8 us
    all_gather x1, waiting for transfers between devices, shards(): key_rows = lax.all_gather(keys_all, 'ctx', axis=0, tiled=True)  42.8 us
  transfers between devices with their start and end apart: 5, of which 5 were waited for; matrix products, arithmetic and copies ran while one was open for 4% of the time, Pallas kernels for 0%

commit v1 on v0

v1 whole, which is shorter than its diff:
```python
import functools

import jax
import jax.numpy as jnp
from jax import lax
from jax.experimental import pallas as pl
from jax.experimental.pallas import tpu as pltpu
from jax.sharding import PartitionSpec as P

HEAD = 128
KV_HEADS = 2
TOP = 8
CAP = 12
ROWS = 128
WIDTH = 2048
FF = 768
DEVS = 128
EPS = 1e-06
THETA = 1000000.0
CHUNK = 1024
BOTH = ("ctx", "exp")
MESH = pl.DeviceIdType.MESH


def rms_scale(v, gain):
    return v * lax.rsqrt(jnp.mean(v * v, axis=-1, keepdims=True) + EPS) * gain


def rope_tables(first):
    half = HEAD // 2
    frequency = THETA ** (-2.0 * jnp.arange(half, dtype=jnp.float32) / HEAD)
    positions = (first + jnp.arange(ROWS)).astype(jnp.float32)
    angles = positions[:, None] * frequency[None, :]
    return jnp.cos(angles), jnp.sin(angles)


def rotate(v, cos, sin):
    half = HEAD // 2
    a, b = v[..., :half], v[..., half:]
    return jnp.concatenate([a * cos - b * sin, b * cos + a * sin], axis=-1)


def place():
    c, e = lax.axis_index("ctx"), lax.axis_index("exp")
    return e // 2, (c // 2) % 2 * 2 + e % 2, c // 4, c % 2


def ids(x, y, z, core):
    return ((z * 2 + y // 2) * 2 + core, x * 2 + y % 2)


def gather_kernel(own, buf, out_sem, x_sem, y_sem, z_sem, f_sem, own_sem):
    x, y, z, c = place()
    yh, yl = y // 2, y % 2
    near = [(lax.rem(x + dx, 4), lax.rem(c + dc, 2)) for dc in range(2) for dx in range(4)]
    ys = [lax.rem(y + d, 4) for d in range(1, 4)]
    zs = [lax.rem(z + d, 4) for d in range(1, 4)]

    barrier = pltpu.get_barrier_semaphore()
    peers = [ids(px, y, z, pc) for px, pc in near[1:]]
    peers += [ids(x, py, z, c) for py in ys] + [ids(x, y, pz, c) for pz in zs]
    for peer in peers:
        pl.semaphore_signal(barrier, inc=1, device_id=peer, device_id_type=MESH)
    pl.semaphore_wait(barrier, len(peers))

    sent = []

    def send(src, dst, slot, sem, peer):
        copy = pltpu.make_async_remote_copy(
            src_ref=src,
            dst_ref=dst,
            send_sem=out_sem.at[slot],
            recv_sem=sem,
            device_id=peer,
            device_id_type=MESH,
        )
        copy.start()
        sent.append(copy)
        return copy

    mine = pltpu.make_async_copy(own.at[x // 2, c], buf.at[c, z, yh, c, x, yl], own_sem)
    mine.start()
    first = []
    for i, (px, pc) in enumerate(near):
        if i:
            first.append(
                send(
                    own.at[px // 2, pc],
                    buf.at[pc, z, yh, c, x, yl],
                    i - 1,
                    x_sem.at[i - 1],
                    ids(px, y, z, pc),
                )
            )
    for copy in first:
        copy.wait_recv()
    mine.wait()

    low, high = pl.ds(0, 2), pl.ds(2, 2)
    every2, every4 = pl.ds(0, 2), pl.ds(0, 4)
    a1 = buf.at[c, z, yh, every2, low, yl]
    b1 = buf.at[c, z, yh, every2, high, yl]
    second_a = [send(a1, a1, 7 + i, y_sem.at[i], ids(x, ys[i], z, c)) for i in range(3)]
    second_b = [send(b1, b1, 10 + i, z_sem.at[i], ids(x, y, zs[i], c)) for i in range(3)]
    for copy in second_a + second_b:
        copy.wait_recv()

    a2 = buf.at[c, z, every2, every2, low, every2]
    b2 = buf.at[c, every4, yh, every2, high, yl]
    third_a = [send(a2, a2, 13 + i, z_sem.at[3 + i], ids(x, y, zs[i], c)) for i in range(3)]
    third_b = [send(b2, b2, 16 + i, y_sem.at[3 + i], ids(x, ys[i], z, c)) for i in range(3)]
    other = ids(x, y, z, 1 - c)
    handed = [send(a2, a2, 19, f_sem.at[0], other), send(b2, b2, 20, f_sem.at[1], other)]
    for i in range(3):
        third_a[i].wait_recv()
        part = buf.at[c, lax.rem(z + 3 - i, 4), every2, every2, low, every2]
        handed.append(send(part, part, 21 + i, f_sem.at[2 + i], other))
        third_b[i].wait_recv()
        py = lax.rem(y + 3 - i, 4)
        part = buf.at[c, every4, py // 2, every2, high, py % 2]
        handed.append(send(part, part, 24 + i, f_sem.at[5 + i], other))
    for copy in handed:
        copy.wait_recv()
    for copy in sent:
        copy.wait_send()


def gather_kv(own):
    return pl.pallas_call(
        gather_kernel,
        out_shape=jax.ShapeDtypeStruct((2, 4, 2, 2, 4, 2, ROWS, HEAD), jnp.bfloat16),
        in_specs=[pl.BlockSpec(memory_space=pl.ANY)],
        out_specs=pl.BlockSpec(memory_space=pl.ANY),
        scratch_shapes=[
            pltpu.SemaphoreType.DMA((27,)),
            pltpu.SemaphoreType.DMA((7,)),
            pltpu.SemaphoreType.DMA((6,)),
            pltpu.SemaphoreType.DMA((6,)),
            pltpu.SemaphoreType.DMA((8,)),
            pltpu.SemaphoreType.DMA,
        ],
        compiler_params=pltpu.CompilerParams(collective_id=0, has_side_effects=True),
    )(own)


def attend_kernel(block_ref, q_ref, k_ref, v_ref, o_ref, qe, acc, top):
    scale = HEAD ** (-0.5) * 1.4426950408889634
    heads = q_ref.shape[1]
    rows = heads * ROWS
    sub = 256
    for part in range(2):
        block = block_ref[part]
        q = q_ref[part].reshape(rows, HEAD).astype(jnp.float32) * scale
        q_hi = q.astype(jnp.bfloat16)
        qe[:, :HEAD] = q_hi
        qe[:, HEAD:] = (q - q_hi.astype(jnp.float32)).astype(jnp.bfloat16)
        acc[...] = jnp.zeros_like(acc)
        top[...] = jnp.full_like(top, -1e30)

        def step(j, masked):
            first = pl.multiple_of(j * CHUNK, CHUNK)
            k = k_ref[pl.ds(first, CHUNK), :]
            v = v_ref[pl.ds(first, CHUNK), :]
            ke = jnp.concatenate([k, k], axis=1)
            ve = jnp.concatenate([v, jnp.ones_like(v)], axis=1)
            for r in range(rows // sub):
                here = pl.ds(r * sub, sub)
                s = lax.dot_general(
                    qe[here, :], ke, (((1,), (1,)), ((), ())), preferred_element_type=jnp.float32
                )
                if masked:
                    row = lax.broadcasted_iota(jnp.int32, s.shape, 0) % ROWS + block * ROWS
                    col = lax.broadcasted_iota(jnp.int32, s.shape, 1) + first
                    s = jnp.where(col <= row, s, -1e30)
                old = top[here, :]
                new = jnp.maximum(old, jnp.max(s, axis=1, keepdims=True))
                top[here, :] = new
                weights = jnp.exp2(s - new[:, :1]).astype(jnp.bfloat16)
                fade = jnp.exp2(old - new)
                o = jnp.dot(weights, ve, preferred_element_type=jnp.float32)
                acc[here, :] = acc[here, :] * jnp.concatenate([fade, fade], axis=1) + o

        whole = block * ROWS // CHUNK

        def body(j, _):
            step(j, False)
            return 0

        lax.fori_loop(0, whole, body, 0)
        step(whole, True)
        for h in range(heads):
            here = pl.ds(h * ROWS, ROWS)
            o_ref[part * ROWS : (part + 1) * ROWS, h * HEAD : (h + 1) * HEAD] = (
                acc[here, :HEAD] / acc[here, HEAD:]
            ).astype(jnp.bfloat16)


def attend(blocks, q, k, v):
    heads = q.shape[1]
    rows = heads * ROWS
    vmem = pl.BlockSpec(memory_space=pltpu.VMEM)
    return pl.pallas_call(
        attend_kernel,
        out_shape=jax.ShapeDtypeStruct((2 * ROWS, heads * HEAD), jnp.bfloat16),
        in_specs=[pl.BlockSpec(memory_space=pltpu.SMEM), vmem, vmem, vmem],
        out_specs=vmem,
        scratch_shapes=[
            pltpu.VMEM((rows, 2 * HEAD), jnp.bfloat16),
            pltpu.VMEM((rows, 2 * HEAD), jnp.float32),
            pltpu.VMEM((rows, HEAD), jnp.float32),
        ],
        compiler_params=pltpu.CompilerParams(vmem_limit_bytes=40 << 20),
        cost_estimate=pl.CostEstimate(
            flops=2 * 2 * 17 * CHUNK * rows * 256, bytes_accessed=10 << 20, transcendentals=17 << 20
        ),
    )(blocks, q, k, v)


GROUP = 16
STEP = 32


def sort_matrix(turned):
    r = lax.broadcasted_iota(jnp.int32, (256, 256), 1 if turned else 0)
    j = lax.broadcasted_iota(jnp.int32, (256, 256), 0 if turned else 1)
    same = (r // 64 == j // 4 % 4) & (r // 4 % 16 == j // 16) & (r % 4 == j % 4)
    return jnp.where(same, 1.0, 0.0).astype(jnp.bfloat16)


def expert_kernel(a_ref, wg_ref, wu_ref, wd_ref, o_ref, x_ref, y_ref):
    gather, spread = sort_matrix(False), sort_matrix(True)
    for h in range(STEP // GROUP):
        for k in range(3):
            part = a_ref[h * GROUP : (h + 1) * GROUP, 16 * k : 16 * k + 16, :].reshape(256, 512)
            part = jnp.dot(gather, part, preferred_element_type=jnp.float32).astype(jnp.bfloat16)
            first = (h * 3 + k) * 64
            for q in range(4):
                x_ref[first : first + 64, q * 512 : (q + 1) * 512] = part[q * 64 : (q + 1) * 64]
    x = x_ref[...]
    gate = jnp.dot(x, wg_ref[...], preferred_element_type=jnp.float32)
    up = jnp.dot(x, wu_ref[...], preferred_element_type=jnp.float32)
    hidden = (gate / (1.0 + jnp.exp(-gate)) * up).astype(jnp.bfloat16)
    y_ref[...] = jnp.dot(hidden, wd_ref[...], preferred_element_type=jnp.float32).astype(
        jnp.bfloat16
    )
    for h in range(STEP // GROUP):
        for k in range(3):
            first = (h * 3 + k) * 64
            part = jnp.concatenate(
                [y_ref[first : first + 64, q * 512 : (q + 1) * 512] for q in range(4)], axis=0
            )
            part = jnp.dot(spread, part, preferred_element_type=jnp.float32).astype(jnp.bfloat16)
            o_ref[h * GROUP : (h + 1) * GROUP, 16 * k : 16 * k + 16, :] = part.reshape(
                GROUP, 16, 512
            )


def experts(arrived, wg, wu, wd):
    rows = STEP * CAP
    once = pl.Buffered(1)
    return pl.pallas_call(
        expert_kernel,
        grid=(DEVS // STEP,),
        out_shape=jax.ShapeDtypeStruct(arrived.shape, jnp.bfloat16),
        in_specs=[
            pl.BlockSpec((STEP, 48, 512), lambda i: (i, 0, 0)),
            pl.BlockSpec((WIDTH, FF), lambda i: (0, 0), pipeline_mode=once),
            pl.BlockSpec((WIDTH, FF), lambda i: (0, 0), pipeline_mode=once),
            pl.BlockSpec((FF, WIDTH), lambda i: (0, 0), pipeline_mode=once),
        ],
        out_specs=pl.BlockSpec((STEP, 48, 512), lambda i: (i, 0, 0)),
        scratch_shapes=[
            pltpu.VMEM((rows, WIDTH), jnp.bfloat16),
            pltpu.VMEM((rows, WIDTH), jnp.bfloat16),
        ],
        compiler_params=pltpu.CompilerParams(vmem_limit_bytes=40 << 20),
        cost_estimate=pl.CostEstimate(
            flops=6 * DEVS * CAP * WIDTH * FF, bytes_accessed=22 << 20, transcendentals=0
        ),
    )(arrived, wg, wu, wd)


def shards(
    tokens,
    ln1_gain,
    w_query,
    key_weight,
    value_weight,
    q_gain,
    k_gain,
    w_out,
    ln2_gain,
    expert_ids,
    route_weights,
    w_gate,
    w_up,
    w_down,
):
    f32, bf16 = jnp.float32, jnp.bfloat16
    me = lax.axis_index("ctx") * 8 + lax.axis_index("exp")
    core = lax.axis_index("ctx") % 2
    partner = [(i, DEVS - 1 - i) for i in range(DEVS)]

    def across(turn):
        return [(i, i ^ turn) for i in range(8)]

    siblings = [(i, i ^ 1) for i in range(16)]

    q_half = lax.dynamic_slice_in_dim(w_query, core * HEAD, HEAD, 1)
    q_got = [lax.ppermute(q_half, "exp", across(t)) for t in (1, 2, 3)]
    q_other = [lax.ppermute(w, "ctx", siblings) for w in q_got]

    inputs32 = tokens.astype(f32)
    normed = rms_scale(inputs32, ln1_gain).astype(bf16)
    normed_partner = lax.ppermute(normed, BOTH, partner)
    cos, sin = rope_tables(me * ROWS)
    cos_p, sin_p = rope_tables((DEVS - 1 - me) * ROWS)

    kv = jnp.dot(
        normed, jnp.concatenate([key_weight, value_weight], axis=1), preferred_element_type=f32
    )
    both = []
    for g in range(KV_HEADS):
        k = rotate(rms_scale(kv[:, g * HEAD : (g + 1) * HEAD], k_gain), cos, sin).astype(bf16)
        v = kv[:, (KV_HEADS + g) * HEAD : (KV_HEADS + g + 1) * HEAD].astype(bf16)
        both.append(jnp.stack([k, v]))
    gathered = gather_kv(jnp.stack(both)).reshape(2, DEVS * ROWS, HEAD)

    weights = jnp.concatenate([w_query] + q_got + q_other, axis=1)
    heads = weights.shape[1] // HEAD

    def queries_of(rows, cos, sin):
        q = jnp.dot(rows, weights, preferred_element_type=f32)
        q = q.reshape(ROWS, heads, HEAD).transpose(1, 0, 2)
        return rotate(rms_scale(q, q_gain), cos, sin).astype(bf16)

    queries = jnp.stack([queries_of(normed, cos, sin), queries_of(normed_partner, cos_p, sin_p)])
    blocks = jnp.stack([me, DEVS - 1 - me]).astype(jnp.int32)
    attended = attend(blocks, queries, gathered[0], gathered[1])

    o_half = lax.dynamic_slice_in_dim(w_out, core * HEAD, HEAD, 0)
    o_got = [lax.ppermute(o_half, "exp", across(t)) for t in (1, 2, 3)]
    o_other = [lax.ppermute(w, "ctx", siblings) for w in o_got]
    out_weights = jnp.concatenate([w_out] + o_got + o_other, axis=0)
    theirs = jnp.dot(attended[ROWS:], out_weights, preferred_element_type=f32).astype(bf16)
    theirs = lax.ppermute(theirs, BOTH, partner)
    mine = jnp.dot(attended[:ROWS], out_weights, preferred_element_type=f32)
    residual = (inputs32 + (mine + theirs.astype(f32))).astype(bf16)
    normed2 = rms_scale(residual.astype(f32), ln2_gain).astype(bf16)

    chosen = expert_ids[:, :, None] == jnp.arange(DEVS)[None, None, :]
    counts = jnp.any(chosen, axis=1)
    before = jnp.arange(ROWS)[:, None] > jnp.arange(ROWS)[None, :]
    rank = jnp.dot(before.astype(bf16), counts.astype(bf16), preferred_element_type=f32)
    slots = jnp.where(counts, rank, -1.0).T
    route = jnp.sum(
        jnp.where(chosen, (route_weights.astype(f32) / 1024.0)[:, :, None], 0.0), axis=1
    ).T
    row = jnp.arange(48)
    row_slot = (row // 16 * 4 + row % 4).astype(f32)
    row_part = row // 4 % 4
    hot = (jnp.tile(slots, (1, 4))[:, None, :] == row_slot[None, :, None]) & (
        row_part[None, :, None] == (jnp.arange(512) // ROWS)[None, None, :]
    )
    dispatch = hot.astype(bf16).reshape(DEVS * 48, 512)
    combine = (
        jnp.where(hot, jnp.tile(route, (1, 4))[:, None, :], 0.0)
        .astype(bf16)
        .reshape(DEVS * 48, 512)
    )
    parts = normed2.reshape(ROWS, 4, 512).transpose(1, 0, 2).reshape(512, 512)
    outgoing = jnp.dot(dispatch, parts, preferred_element_type=f32).astype(bf16)
    arrived = lax.all_to_all(outgoing, BOTH, split_axis=0, concat_axis=0, tiled=True)
    produced = experts(arrived.reshape(DEVS, 48, 512), w_gate[0], w_up[0], w_down[0])
    returned = lax.all_to_all(
        produced.reshape(DEVS * 48, 512), BOTH, split_axis=0, concat_axis=0, tiled=True
    )
    mixture = lax.dot_general(
        combine, returned, (((0,), (0,)), ((), ())), preferred_element_type=f32
    )
    mixture = mixture.reshape(4, ROWS, 512).transpose(1, 0, 2).reshape(ROWS, WIDTH)
    return (residual.astype(f32) + mixture).astype(bf16)


def solution(mesh):
    two = P(BOTH, None)
    three = P(BOTH, None, None)
    in_specs = (
        two,
        P(),
        P(None, "exp"),
        P(),
        P(),
        P(),
        P(),
        P("exp", None),
        P(),
        two,
        two,
        three,
        three,
        three,
    )
    return jax.shard_map(shards, mesh=mesh, in_specs=in_specs, out_specs=two, check_vma=False)
```

time: 811 us -> 382 us (0.47)
  waiting for transfers between devices: 524 us -> 85.1 us
  Pallas kernels: 0 us -> 110 us
  matrix products: 63.1 us -> 19.3 us
  blocking collectives: 107 us -> 79.5 us
  starting transfers between devices: 7.07 us -> 29 us
  local copies, waits for them, and re-layouts: 60.7 us -> 42.5 us
  between operations: 13.7 us -> 0.53 us
  other arithmetic: 24.9 us -> 14.5 us
    reduce_scatter x1 -> x0, waiting for transfers between devices: 244 us -> none  [shards(): lax.psum_scatter(jnp.dot(attended, w_out, preferred_element_type=jnp.floa...]
    all_gather x3 -> x0, waiting for transfers between devices: 182 us -> none  [the longest x1 90.7 us: shards(): lax.all_gather(normed_input, 'exp', axis=0, tiled=True)]
    pallas_call x0 -> x3, Pallas kernels: none -> 110 us  [the longest x1 55.1 us: gather_kv(): pl.pallas_call(gather_kernel, out_shape=jax.ShapeDtypeStruct((2, 4, 2, 2,...]
    dot_general x13 -> x8, matrix products: 63.1 us -> 19.3 us  [the longest x1 7.45 us: shards(): lax.dot_general(combine, returned, (((0,), (0,)), ((), ())), preferred_el...]
    all_to_all x1, waiting for transfers between devices: 97.5 us -> 59.9 us  [shards(): lax.all_to_all(produced.reshape(DEVS * 48, 512), BOTH, split_axis=0, conc...]
    all_to_all x1, blocking collectives: 107 us -> 79.5 us  [shards(): lax.all_to_all(outgoing, BOTH, split_axis=0, concat_axis=0, tiled=True)]
    ppermute x0 -> x14, waiting for transfers between devices: none -> 25.1 us  [the longest x1 13.4 us: shards(): theirs = lax.ppermute(theirs, BOTH, partner)]
    reshape x3 -> x4, local copies, waits for them, and re-layouts: 23.8 us -> 0.51 us  [the longest x2 0.39 us: queries_of(): q = q.reshape(ROWS, heads, HEAD).transpose(1, 0, 2)]
  transfers between devices with their start and end apart: 5 -> 15, of which waited for: 5 -> 4; matrix products, arithmetic and copies ran while one was open for 4% -> 15% of each run, Pallas kernels for 0% -> 23%
where the time goes in v1:
time: 382 us; the launch traced here: 380 us
  Pallas kernels  110 us (29%)
  waiting for transfers between devices  85.1 us (22%)
  blocking collectives  79.5 us (21%)
  local copies, waits for them, and re-layouts  42.5 us (11%)
  starting transfers between devices  29 us (8%)
  matrix products  19.3 us (5%)
  other arithmetic  14.5 us (4%)
    all_to_all x1, blocking collectives, shards(): lax.all_to_all(outgoing, BOTH, split_axis=0, concat_axis=0, tiled=True)  79.5 us
    all_to_all x1, waiting for transfers between devices, shards(): lax.all_to_all(produced.reshape(DEVS * 48, 512), BOTH, split_axis=0, conc...  59.9 us
    pallas_call x1, Pallas kernels, gather_kv(): pl.pallas_call(gather_kernel, out_shape=jax.ShapeDtypeStruct((2, 4, 2, 2,...  55.1 us
    pallas_call x1, Pallas kernels, attend(): pl.pallas_call(attend_kernel, out_shape=jax.ShapeDtypeStruct((2 * ROWS, h...  33 us
    pallas_call x1, Pallas kernels, experts(): pl.pallas_call(expert_kernel, grid=(DEVS // STEP,), out_shape=jax.ShapeDt...  21.6 us
    unnamed x49, local copies, waits for them, and re-layouts  20.9 us
    ppermute x1, waiting for transfers between devices, shards(): theirs = lax.ppermute(theirs, BOTH, partner)  13.4 us
    ppermute x3, waiting for transfers between devices, shards(): o_got = [lax.ppermute(o_half, 'exp', across(t)) for t in (1, 2, 3)]  11.7 us
  transfers between devices with their start and end apart: 15, of which 4 were waited for; matrix products, arithmetic and copies ran while one was open for 15% of the time, Pallas kernels for 23%

profile of v1, /device:TPU:1, one launch (start us, length us, event | category | flops | bytes accessed | tf_op | source)
XLA Modules:
  0.0 380.1 jit_solution(5231420890638064462)
XLA Ops:
  0.0 2.0 constant_dynamic-slice_fusion.1
  2.0 2.1 collective-permute-start
  4.2 1.2 collective-permute-start.1
  5.4 1.2 fusion.9
  6.6 1.2 fusion.11
  7.9 10.0 %collective-permute-start.6 = (bf16[128,2048]{1,0:T(8,128)(2,1)S(1)}, bf16[128,2048]{1,0:T(8,128)(2,1)S(1)}, u32[]{:S(2)}, u32[]{:S(2)}) collective-permute-start(bf16[128,2048]{1,0:T(8,128)(2,1)S(1)} %fusion.11), channel_id=1, source_target_pairs={{0,127},{1,126},{2,125},{3,124},{4,123},{5,122},{6,121},{7,120},{8... | collective-permute-start | bytes 1572872 | tf_op jit(solution)/shard_map/ppermute | solution.py:315
  17.9 1.9 constant_dynamic-slice_fusion
  19.8 1.2 constant_dynamic-update-slice_fusion.6
  21.0 1.1 constant_dynamic-update-slice_fusion.13
  23.5 0.7 pad_maximum_fusion.own
  24.1 55.1 %shard_map.136 = bf16[2,4,2,2,4,2,128,128]{7,6,5,4,3,2,1,0:T(8,128)(2,1)} custom-call(bf16[2,2,128,128]{3,2,1,0:T(8,128)(2,1)} %pad_maximum_fusion.own), custom_call_target="tpu_custom_call" | custom-call | tf_op jit(solution)/shard_map/pallas_call | solution.py:129
  79.3 6.0 %fusion.52 = (bf16[1,4,2,2,4,2,128,128]{7,6,5,4,3,2,1,0:T(8,128)(2,1)}, bf16[1,4,2,2,4,2,128,128]{7,6,5,4,3,2,1,0:T(8,128)(2,1)}) fusion(bf16[2,4,2,2,4,2,128,128]{7,6,5,4,3,2,1,0:T(8,128)(2,1)} %shard_map.136), kind=kLoop, calls=%fused_computation.135 | loop fusion | bytes 16777216 | tf_op jit(solution)/shard_map/slice | solution.py:339
  86.2 2.8 collective-permute-start.8
  89.0 2.0 constant_dynamic-update-slice_fusion.5
  91.0 1.9 constant_dynamic-update-slice_fusion.4
  93.2 1.9 constant_dynamic-update-slice_fusion.3
  95.3 1.9 constant_dynamic-update-slice_fusion.12
  97.2 4.3 %collective-permute-done.8 = bf16[128,2048]{1,0:T(8,128)(2,1)} collective-permute-done((bf16[128,2048]{1,0:T(8,128)(2,1)}, bf16[128,2048]{1,0:T(8,128)(2,1)}, u32[]{:S(2)}, u32[]{:S(2)}) %collective-permute-start.8) | collective-permute-done | bytes 524320 | tf_op jit(solution)/shard_map/ppermute | solution.py:342
  101.5 0.9 collective-permute-start.5
  102.5 1.9 constant_dynamic-update-slice_fusion.11
  104.4 7.5 %collective-permute-done.9 = bf16[128,2048]{1,0:T(8,128)(2,1)} collective-permute-done((bf16[128,2048]{1,0:T(8,128)(2,1)}, bf16[128,2048]{1,0:T(8,128)(2,1)}, u32[]{:S(2)}, u32[]{:S(2)}) %collective-permute-start.9) | collective-permute-done | bytes 524320 | tf_op jit(solution)/shard_map/ppermute | solution.py:342
  111.8 0.9 collective-permute-start.10
  112.7 1.9 constant_dynamic-update-slice_fusion.10
  114.6 0.9 constant_dynamic-update-slice_fusion.2
  116.0 0.9 constant_dynamic-update-slice_fusion.1
  116.9 0.9 constant_dynamic-update-slice_fusion
  117.8 4.1 %fusion.54 = f32[128,1024]{0,1:T(8,128)S(1)} fusion(bf16[128,2048]{1,0:T(8,128)(2,1)S(1)} %fusion.11, bf16[2048,1024]{1,0:T(8,128)(2,1)} %constant_dynamic-update-slice_fusion), kind=kOutput, calls=%fused_computation.137 | convolution fusion | flops 536870912 | bytes 5242880 | tf_op jit(solution)/shard_map/dot_general | solution.py:333
  122.0 1.8 fusion.55
  125.7 0.8 copy-done
  126.6 2.2 copy-done.1
  128.8 33.0 %shard_map.137 = bf16[256,1024]{1,0:T(8,128)(2,1)S(1)} custom-call(s32[2]{0:T(128)S(1)} %pad_add_fusion.block_ref, bf16[2,8,128,128]{3,2,1,0:T(8,128)(2,1)S(1)} %maximum_maximum_fusion.q_ref, bf16[16384,128]{1,0:T(8,128)(2,1)S(1)} %bitcast.100, bf16[16384,128]{1,0:T(8,128)(2,1)S(1)} %bitcast.99), custom_call_target="tpu_custom_call" | custom-call | flops 18253611008 | bytes 10485760 | tf_op jit(solution)/shard_map/pallas_call | solution.py:202
  161.8 1.1 constant_dynamic-update-slice_fusion.9
  162.9 1.1 constant_dynamic-update-slice_fusion.8
  164.0 1.1 constant_dynamic-update-slice_fusion.7
  165.1 0.7 convolution_convert_fusion.1
  165.9 3.6 collective-permute-start.13
  169.4 2.1 compare_and_fusion
  171.5 13.4 %collective-permute-done.13 = bf16[128,2048]{1,0:T(8,128)(2,1)S(1)} collective-permute-done((bf16[128,2048]{1,0:T(8,128)(2,1)S(1)}, bf16[128,2048]{1,0:T(8,128)(2,1)S(1)}, u32[]{:S(2)}, u32[]{:S(2)}) %collective-permute-start.13) | collective-permute-done | bytes 524320 | tf_op jit(solution)/shard_map/ppermute | solution.py:346
  184.9 1.0 multiply_reduce_fusion
  186.1 3.6 convolution_convert_fusion
  189.8 79.5 %all_to_all.18.a_ref = bf16[128,48,512]{2,1,0:T(8,128)(2,1)} all-to-all(bf16[128,48,512]{2,1,0:T(8,128)(2,1)S(1)} %bitcast.106), channel_id=1, replica_groups=mesh['ctx'=16,'exp'=8] {'ctx','exp'}, dimensions={0} | all-to-all | bytes 12582912 | tf_op jit(solution)/shard_map/all_to_all | solution.py:373
  269.3 21.6 %shard_map.138 = bf16[128,48,512]{2,1,0:T(8,128)(2,1)} custom-call(bf16[128,48,512]{2,1,0:T(8,128)(2,1)} %all_to_all.18.a_ref, bf16[2048,768]{1,0:T(8,128)(2,1)S(1)} %bitcast.101, bf16[2048,768]{1,0:T(8,128)(2,1)S(1)} %bitcast.102, bf16[768,2048]{1,0:T(8,128)(2,1)S(1)} %bitcast.103), custom_call_target="tpu_custom_call" | custom-call | flops 14495514624 | bytes 23068672 | tf_op jit(solution)/shard_map/pallas_call | solution.py:261
  290.9 6.4 %all-to-all-start.1 = ((bf16[128,48,512]{2,1,0:T(8,128)(2,1)}), bf16[128,48,512]{2,1,0:T(8,128)(2,1)}, u32[]{:S(2)}, u32[]{:S(2)}) async-start(bf16[128,48,512]{2,1,0:T(8,128)(2,1)} %shard_map.138), calls=%async_computation.1 | async-start | bytes 12582912 | tf_op jit(solution)/shard_map/all_to_all | solution.py:375
  298.1 5.0 %fusion = bf16[6144,512]{1,0:T(8,128)(2,1)} fusion(bf16[128,512]{1,0:T(8,128)(2,1)S(1)} %bitcast.115, f32[6144]{0:T(1024)S(1)} %eq.80, f32[128,512]{1,0:T(8,128)S(1)} %bitcast.110, pred[48,512]{1,0:T(8,128)(4,1)S(1)} %broadcast_compare_fusion), kind=kLoop, calls=%fused_computation.1 | loop fusion | flops 9437184 | bytes 6733824 | tf_op jit(solution)/shard_map/convert_element_type | solution.py:368
  303.1 8.6 %copy.41 = bf16[512,6144]{1,0:T(8,128)(2,1)} copy(bf16[512,6144]{0,1:T(8,128)(2,1)} %bitcast.104) | data formatting | bytes 12582912 | tf_op jit(solution)/shard_map/dot_general | solution.py:378
  311.7 59.9 %all-to-all-done.1 = bf16[128,48,512]{2,1,0:T(8,128)(2,1)} async-done(((bf16[128,48,512]{2,1,0:T(8,128)(2,1)}), bf16[128,48,512]{2,1,0:T(8,128)(2,1)}, u32[]{:S(2)}, u32[]{:S(2)}) %all-to-all-start.1) | async-done | bytes 6291488 | tf_op jit(solution)/shard_map/all_to_all | solution.py:375
  371.7 7.5 %convolution_bitcast_fusion = f32[4,16,8,512]{3,2,1,0:T(8,128)S(1)} fusion(bf16[4,128,6144]{2,1,0:T(8,128)(2,1)} %bitcast.105, bf16[6144,512,1]{1,0,2:T(8,128)(2,1)} %bitcast.35), kind=kOutput, calls=%fused_computation.17 | convolution fusion | flops 3221225472 | bytes 13631488 | tf_op jit(solution)/shard_map/dot_general | solution.py:378
  379.2 0.9 add_convert_fusion
  (93 shorter events, 6.3 us)
Async XLA Ops:
  0.0 19.8 %copy-start.8 = (bf16[2048,256]{1,0:T(8,128)(2,1)S(1)}, bf16[2048,256]{1,0:T(8,128)(2,1)}, u32[]{:S(2)}) copy-start(bf16[2048,256]{1,0:T(8,128)(2,1)} %param.16) | copy-start | bytes 3145732
  0.0 21.0 %copy-start.9 = (bf16[256,2048]{1,0:T(8,128)(2,1)S(1)}, bf16[256,2048]{1,0:T(8,128)(2,1)}, u32[]{:S(2)}) copy-start(bf16[256,2048]{1,0:T(8,128)(2,1)} %param.21) | copy-start | bytes 3145732
  0.0 22.0 %copy-start.15 = (bf16[2048,256]{1,0:T(8,128)(2,1)S(1)}, bf16[2048,256]{1,0:T(8,128)(2,1)}, u32[]{:S(2)}) copy-start(bf16[2048,256]{1,0:T(8,128)(2,1)} %param.18) | copy-start | bytes 3145732
  0.0 22.0 %copy-start.16 = (bf16[2048,256]{1,0:T(8,128)(2,1)S(1)}, bf16[2048,256]{1,0:T(8,128)(2,1)}, u32[]{:S(2)}) copy-start(bf16[2048,256]{1,0:T(8,128)(2,1)} %param.17) | copy-start | bytes 3145732
  2.0 84.1 %collective-permute-start = (bf16[2048,128]{1,0:T(8,128)(2,1)}, bf16[2048,128]{1,0:T(8,128)(2,1)}, u32[]{:S(2)}, u32[]{:S(2)}) collective-permute-start(bf16[2048,128]{1,0:T(8,128)(2,1)} %constant_dynamic-slice_fusion.1), channel_id=1, source_target_pairs={{0,1},{1,0},{2,3},{3,2},{4,5},{5,4},{6,7},{7,6},{8,9},{9,8},{10,11... | collective-permute-start | bytes 1572872 | tf_op jit(solution)/shard_map/ppermute | solution.py:310
  4.2 86.8 %collective-permute-start.1 = (bf16[2048,128]{1,0:T(8,128)(2,1)}, bf16[2048,128]{1,0:T(8,128)(2,1)}, u32[]{:S(2)}, u32[]{:S(2)}) collective-permute-start(bf16[2048,128]{1,0:T(8,128)(2,1)} %constant_dynamic-slice_fusion.1), channel_id=1, source_target_pairs={{0,2},{1,3},{2,0},{3,1},{4,6},{5,7},{6,4},{7,5},{8,10},{9,11},{10,... | collective-permute-start | bytes 1572872 | tf_op jit(solution)/shard_map/ppermute | solution.py:310
  5.4 87.5 %collective-permute-start.2 = (bf16[2048,128]{1,0:T(8,128)(2,1)}, bf16[2048,128]{1,0:T(8,128)(2,1)}, u32[]{:S(2)}, u32[]{:S(2)}) collective-permute-start(bf16[2048,128]{1,0:T(8,128)(2,1)} %constant_dynamic-slice_fusion.1), channel_id=1, source_target_pairs={{0,3},{1,2},{2,1},{3,0},{4,7},{5,6},{6,5},{7,4},{8,11},{9,10},{10,... | collective-permute-start | bytes 1572872 | tf_op jit(solution)/shard_map/ppermute | solution.py:310
  7.9 114.1 %collective-permute-start.6 = (bf16[128,2048]{1,0:T(8,128)(2,1)S(1)}, bf16[128,2048]{1,0:T(8,128)(2,1)S(1)}, u32[]{:S(2)}, u32[]{:S(2)}) collective-permute-start(bf16[128,2048]{1,0:T(8,128)(2,1)S(1)} %fusion.11), channel_id=1, source_target_pairs={{0,127},{1,126},{2,125},{3,124},{4,123},{5,122},{6,121},{7,120},{8... | collective-permute-start | bytes 1572872 | tf_op jit(solution)/shard_map/ppermute | solution.py:315
  19.8 2.9 copy-start.13
  19.8 75.4 %collective-permute-start.7 = (bf16[128,2048]{1,0:T(8,128)(2,1)}, bf16[128,2048]{1,0:T(8,128)(2,1)}, u32[]{:S(2)}, u32[]{:S(2)}) collective-permute-start(bf16[128,2048]{1,0:T(8,128)(2,1)} %constant_dynamic-slice_fusion), channel_id=1, source_target_pairs={{0,1},{1,0},{2,3},{3,2},{4,5},{5,4},{6,7},{7,6},{8,9},{9,8},{10,11... | collective-permute-start | bytes 1572872 | tf_op jit(solution)/shard_map/ppermute | solution.py:342
  79.2 6.0 %copy-start.11 = (s32[128,8]{0,1:T(8,128)S(1)}, s32[128,8]{0,1:T(8,128)}, u32[]{:S(2)}) copy-start(s32[128,8]{0,1:T(8,128)} %param.23) | copy-start | bytes 12292
  86.2 15.3 %collective-permute-start.8 = (bf16[128,2048]{1,0:T(8,128)(2,1)}, bf16[128,2048]{1,0:T(8,128)(2,1)}, u32[]{:S(2)}, u32[]{:S(2)}) collective-permute-start(bf16[128,2048]{1,0:T(8,128)(2,1)} %constant_dynamic-slice_fusion), channel_id=1, source_target_pairs={{0,2},{1,3},{2,0},{3,1},{4,6},{5,7},{6,4},{7,5},{8,10},{9,11},{10,... | collective-permute-start | bytes 1572872 | tf_op jit(solution)/shard_map/ppermute | solution.py:342
  91.0 20.9 %collective-permute-start.9 = (bf16[128,2048]{1,0:T(8,128)(2,1)}, bf16[128,2048]{1,0:T(8,128)(2,1)}, u32[]{:S(2)}, u32[]{:S(2)}) collective-permute-start(bf16[128,2048]{1,0:T(8,128)(2,1)} %constant_dynamic-slice_fusion), channel_id=1, source_target_pairs={{0,3},{1,2},{2,1},{3,0},{4,7},{5,6},{6,5},{7,4},{8,11},{9,10},{10,... | collective-permute-start | bytes 1572872 | tf_op jit(solution)/shard_map/ppermute | solution.py:342
  92.9 21.7 %collective-permute-start.3 = (bf16[2048,128]{1,0:T(8,128)(2,1)}, bf16[2048,128]{1,0:T(8,128)(2,1)S(1)}, u32[]{:S(2)}, u32[]{:S(2)}) collective-permute-start(bf16[2048,128]{1,0:T(8,128)(2,1)} %collective-permute-done), channel_id=1, source_target_pairs={{0,8},{8,0},{16,24},{24,16},{32,40},{40,32},{48,56},{56,48},{64,72... | collective-permute-start | bytes 1572872 | tf_op jit(solution)/shard_map/ppermute | solution.py:311
  95.2 20.3 %collective-permute-start.4 = (bf16[2048,128]{1,0:T(8,128)(2,1)}, bf16[2048,128]{1,0:T(8,128)(2,1)S(1)}, u32[]{:S(2)}, u32[]{:S(2)}) collective-permute-start(bf16[2048,128]{1,0:T(8,128)(2,1)} %collective-permute-done.1), channel_id=1, source_target_pairs={{0,8},{8,0},{16,24},{24,16},{32,40},{40,32},{48,56},{56,48},{64,72... | collective-permute-start | bytes 1572872 | tf_op jit(solution)/shard_map/ppermute | solution.py:311
  101.5 15.4 %collective-permute-start.5 = (bf16[2048,128]{1,0:T(8,128)(2,1)}, bf16[2048,128]{1,0:T(8,128)(2,1)S(1)}, u32[]{:S(2)}, u32[]{:S(2)}) collective-permute-start(bf16[2048,128]{1,0:T(8,128)(2,1)} %collective-permute-done.2), channel_id=1, source_target_pairs={{0,8},{8,0},{16,24},{24,16},{32,40},{40,32},{48,56},{56,48},{64,72... | collective-permute-start | bytes 1572872 | tf_op jit(solution)/shard_map/ppermute | solution.py:311
  111.8 50.0 %collective-permute-start.10 = (bf16[128,2048]{1,0:T(8,128)(2,1)}, bf16[128,2048]{1,0:T(8,128)(2,1)}, u32[]{:S(2)}, u32[]{:S(2)}) collective-permute-start(bf16[128,2048]{1,0:T(8,128)(2,1)} %collective-permute-done.7), channel_id=1, source_target_pairs={{0,8},{8,0},{16,24},{24,16},{32,40},{40,32},{48,56},{56,48},{64,72... | collective-permute-start | bytes 1572872 | tf_op jit(solution)/shard_map/ppermute | solution.py:343
  114.6 48.3 %collective-permute-start.11 = (bf16[128,2048]{1,0:T(8,128)(2,1)}, bf16[128,2048]{1,0:T(8,128)(2,1)}, u32[]{:S(2)}, u32[]{:S(2)}) collective-permute-start(bf16[128,2048]{1,0:T(8,128)(2,1)} %collective-permute-done.8), channel_id=1, source_target_pairs={{0,8},{8,0},{16,24},{24,16},{32,40},{40,32},{48,56},{56,48},{64,72... | collective-permute-start | bytes 1572872 | tf_op jit(solution)/shard_map/ppermute | solution.py:343
  115.5 48.5 %collective-permute-start.12 = (bf16[128,2048]{1,0:T(8,128)(2,1)}, bf16[128,2048]{1,0:T(8,128)(2,1)}, u32[]{:S(2)}, u32[]{:S(2)}) collective-permute-start(bf16[128,2048]{1,0:T(8,128)(2,1)} %collective-permute-done.9), channel_id=1, source_target_pairs={{0,8},{8,0},{16,24},{24,16},{32,40},{40,32},{48,56},{56,48},{64,72... | collective-permute-start | bytes 1572872 | tf_op jit(solution)/shard_map/ppermute | solution.py:343
  117.8 4.1 %copy-start.5 = (bf16[2048,1024]{1,0:T(8,128)(2,1)S(1)}, bf16[2048,1024]{1,0:T(8,128)(2,1)}, u32[]{:S(2)}) copy-start(bf16[2048,1024]{1,0:T(8,128)(2,1)} %constant_dynamic-update-slice_fusion) | copy-start | bytes 12582916
  121.9 2.7 copy-start.14
  124.4 2.2 copy-start
  126.6 2.2 copy-start.1
  128.8 33.1 %copy-start.6 = (bf16[1024,2048]{1,0:T(8,128)(2,1)S(1)}, bf16[1024,2048]{1,0:T(8,128)(2,1)}, u32[]{:S(2)}) copy-start(bf16[1024,2048]{1,0:T(8,128)(2,1)} %constant_dynamic-update-slice_fusion.10) | copy-start | bytes 12582916
  165.1 19.8 %copy-start.7 = (bf16[128,2048]{1,0:T(8,128)(2,1)S(1)}, bf16[128,2048]{1,0:T(8,128)(2,1)}, u32[]{:S(2)}) copy-start(bf16[128,2048]{1,0:T(8,128)(2,1)} %param.14) | copy-start | bytes 1572868
  165.9 19.0 %collective-permute-start.13 = (bf16[128,2048]{1,0:T(8,128)(2,1)S(1)}, bf16[128,2048]{1,0:T(8,128)(2,1)S(1)}, u32[]{:S(2)}, u32[]{:S(2)}) collective-permute-start(bf16[128,2048]{1,0:T(8,128)(2,1)S(1)} %convolution_convert_fusion.1), channel_id=1, source_target_pairs={{0,127},{1,126},{2,125},{3,124},{4,123},{5,122},{6,121},{7,120},{8... | collective-permute-start | bytes 1572872 | tf_op jit(solution)/shard_map/ppermute | solution.py:346
  169.4 16.4 %copy-start.10 = (f32[2048]{0:T(1024)S(1)}, f32[2048]{0:T(1024)}, u32[]{:S(2)}) copy-start(f32[2048]{0:T(1024)} %param.22) | copy-start | bytes 24580
  189.7 79.5 %copy-start.2 = (bf16[1,2048,768]{2,1,0:T(8,128)(2,1)S(1)}, bf16[1,2048,768]{2,1,0:T(8,128)(2,1)}, u32[]{:S(2)}) copy-start(bf16[1,2048,768]{2,1,0:T(8,128)(2,1)} %param.25) | copy-start | bytes 9437188
  189.8 79.5 %copy-start.3 = (bf16[1,2048,768]{2,1,0:T(8,128)(2,1)S(1)}, bf16[1,2048,768]{2,1,0:T(8,128)(2,1)}, u32[]{:S(2)}) copy-start(bf16[1,2048,768]{2,1,0:T(8,128)(2,1)} %param.26) | copy-start | bytes 9437188
  189.8 79.5 %copy-start.4 = (bf16[1,768,2048]{2,1,0:T(8,128)(2,1)S(1)}, bf16[1,768,2048]{2,1,0:T(8,128)(2,1)}, u32[]{:S(2)}) copy-start(bf16[1,768,2048]{2,1,0:T(8,128)(2,1)} %param.27) | copy-start | bytes 9437188
  290.9 6.5 %copy-start.12 = (s32[128,8]{0,1:T(8,128)S(1)}, s32[128,8]{0,1:T(8,128)}, u32[]{:S(2)}) copy-start(s32[128,8]{0,1:T(8,128)} %param.24) | copy-start | bytes 12292
  290.9 80.8 %all-to-all-start.1 = ((bf16[128,48,512]{2,1,0:T(8,128)(2,1)}), bf16[128,48,512]{2,1,0:T(8,128)(2,1)}, u32[]{:S(2)}, u32[]{:S(2)}) async-start(bf16[128,48,512]{2,1,0:T(8,128)(2,1)} %shard_map.138), calls=%async_computation.1 | async-start | bytes 12582912 | tf_op jit(solution)/shard_map/all_to_all | solution.py:375

commit v2 on v1

v2 whole, which is shorter than its diff:
```python
import jax
import jax.numpy as jnp
from jax import lax
from jax.experimental import pallas as pl
from jax.experimental.pallas import tpu as pltpu
from jax.sharding import PartitionSpec as P

HEAD = 128
KV_HEADS = 2
QUERY_HEADS = 16
TOP = 8
CAP = 12
ROWS = 128
WIDTH = 2048
FF = 768
DEVS = 128
EPS = 1e-06
THETA = 1000000.0
CHUNK = 1024
BOTH = ("ctx", "exp")
MESH = pl.DeviceIdType.MESH


def rope_tables(first):
    half = HEAD // 2
    frequency = THETA ** (-2.0 * jnp.arange(half, dtype=jnp.float32) / HEAD)
    positions = (first + jnp.arange(ROWS)).astype(jnp.float32)
    angles = positions[:, None] * frequency[None, :]
    return jnp.cos(angles), jnp.sin(angles)


def place():
    c, e = lax.axis_index("ctx"), lax.axis_index("exp")
    return e // 2, (c // 2) % 2 * 2 + e % 2, c // 4, c % 2


def ids(x, y, z, core):
    return ((z * 2 + y // 2) * 2 + core, x * 2 + y % 2)


def norm_rows(v, gain):
    return v * lax.rsqrt(jnp.mean(v * v, axis=-1, keepdims=True) + EPS) * gain


def turn(v, cos, sin):
    return v * cos + pltpu.roll(v, HEAD // 2, 1) * sin


def layer_kernel(
    tokens,
    ln1,
    w_query,
    w_key,
    w_value,
    q_gain,
    k_gain,
    w_out,
    ln2,
    cos,
    sin,
    residual,
    normed2,
    normed,
    own,
    buf,
    wq,
    wo,
    qe,
    acc,
    top,
    attended,
    leaving,
    landing,
    kept,
    out_sem,
    in_sem,
):
    f32, bf16 = jnp.float32, jnp.bfloat16
    x, y, z, c = place()
    yh, yl = y // 2, y % 2
    b = lax.axis_index("ctx") * 8 + lax.axis_index("exp")
    x1, y1 = x + 1 - 2 * (x % 2), y + 1 - 2 * (y % 2)
    near = [(lax.rem(x + dx, 4), lax.rem(c + dc, 2)) for dc in range(2) for dx in range(4)]
    ys = [lax.rem(y + d, 4) for d in range(1, 4)]
    zs = [lax.rem(z + d, 4) for d in range(1, 4)]
    other = ids(x, y, z, 1 - c)
    partner = ids(3 - x, 3 - y, 3 - z, 1 - c)
    beside, along, diagonal = ids(x, y1, z, c), ids(x1, y, z, c), ids(x1, y1, z, c)

    barrier = pltpu.get_barrier_semaphore()
    peers = [ids(px, y, z, pc) for px, pc in near[1:]]
    peers += [ids(x, py, z, c) for py in ys] + [ids(x, y, pz, c) for pz in zs]
    peers += [partner, diagonal]
    for peer in peers:
        pl.semaphore_signal(barrier, inc=1, device_id=peer, device_id_type=MESH)

    sent = []

    def send(src, dst, peer):
        copy = pltpu.make_async_remote_copy(
            src_ref=src,
            dst_ref=dst,
            send_sem=out_sem.at[len(sent)],
            recv_sem=in_sem.at[len(sent)],
            device_id=peer,
            device_id_type=MESH,
        )
        copy.start()
        sent.append(copy)
        return copy

    rows = norm_rows(tokens[...].astype(f32), ln1[...]).astype(bf16)
    normed[0] = rows
    keys = jnp.dot(rows, w_key[...], preferred_element_type=f32)
    values = jnp.dot(rows, w_value[...], preferred_element_type=f32).astype(bf16)
    for g in range(KV_HEADS):
        k = norm_rows(keys[:, g * HEAD : (g + 1) * HEAD], k_gain[...])
        own[g, 0] = turn(k, cos[0], sin[0]).astype(bf16)
        own[g, 1] = values[:, g * HEAD : (g + 1) * HEAD]
    buf[c, z, yh, c, x, yl] = own[x // 2, c]
    pl.semaphore_wait(barrier, len(peers))

    first = []
    for px, pc in near[1:]:
        first.append(
            send(own.at[px // 2, pc], buf.at[pc, z, yh, c, x, yl], ids(px, y, z, pc))
        )
    half = w_query.at[:, pl.ds(pl.multiple_of(c * HEAD, HEAD), HEAD)]
    q1 = send(half, wq.at[0, c], beside)
    q2 = send(half, wq.at[1, c], along)
    swap = send(normed.at[0], normed.at[1], partner)
    for copy in first:
        copy.wait_recv()

    low, high = pl.ds(0, 2), pl.ds(2, 2)
    two, four = pl.ds(0, 2), pl.ds(0, 4)
    a1 = buf.at[c, z, yh, two, low, yl]
    b1 = buf.at[c, z, yh, two, high, yl]
    second = [send(a1, a1, ids(x, py, z, c)) for py in ys]
    second += [send(b1, b1, ids(x, y, pz, c)) for pz in zs]
    for copy in second:
        copy.wait_recv()

    def of_z(pz, part=two):
        return buf.at[c, pz, part, two, low, two]

    def of_y(py, part=four):
        return buf.at[c, part, py // 2, two, high, py % 2]

    up_z, down_z, up_y, down_y = zs[0], zs[2], ys[0], ys[2]
    third = [
        send(of_z(z), of_z(z), ids(x, y, up_z, c)),
        send(of_z(z), of_z(z), ids(x, y, down_z, c)),
        send(of_y(y), of_y(y), ids(x, up_y, z, c)),
        send(of_y(y), of_y(y), ids(x, down_y, z, c)),
    ]
    handed = [send(of_z(z), of_z(z), other), send(of_y(y), of_y(y), other)]
    q1.wait_recv()
    q3 = send(wq.at[0, c], wq.at[2, c], along)
    handed_q = [send(wq.at[0, c], wq.at[0, c], other)]
    q2.wait_recv()
    handed_q.append(send(wq.at[1, c], wq.at[1, c], other))

    third[0].wait_recv()
    part = of_z(down_z, pl.ds(0, 1))
    fourth = [send(part, part, ids(x, y, up_z, c))]
    handed.append(send(of_z(down_z), of_z(down_z), other))
    third[1].wait_recv()
    part = of_z(up_z, pl.ds(1, 1))
    fourth.append(send(part, part, ids(x, y, down_z, c)))
    handed.append(send(of_z(up_z), of_z(up_z), other))
    third[2].wait_recv()
    part = of_y(down_y, pl.ds(0, 2))
    fourth.append(send(part, part, ids(x, up_y, z, c)))
    handed.append(send(of_y(down_y), of_y(down_y), other))
    third[3].wait_recv()
    part = of_y(up_y, pl.ds(2, 2))
    fourth.append(send(part, part, ids(x, down_y, z, c)))
    handed.append(send(of_y(up_y), of_y(up_y), other))

    scale = HEAD ** (-0.5) * 1.4426950408889634

    def queries(index, weights):
        both = jnp.dot(
            normed[...].reshape(2 * ROWS, WIDTH), weights, preferred_element_type=f32
        )
        for h in range(2):
            for p in range(2):
                v = both[p * ROWS : (p + 1) * ROWS, h * HEAD : (h + 1) * HEAD]
                v = turn(norm_rows(v, q_gain[...]), cos[p], sin[p]).astype(bf16)
                v = v.astype(f32) * scale
                v_hi = v.astype(bf16)
                here = pl.ds((index * 2 + h) * ROWS, ROWS)
                qe[p, here, :HEAD] = v_hi
                qe[p, here, HEAD:] = (v - v_hi.astype(f32)).astype(bf16)

    swap.wait_recv()
    queries(0, w_query[...])
    q3.wait_recv()
    handed_q.append(send(wq.at[2, c], wq.at[2, c], other))
    for t in range(2):
        handed_q[t].wait_recv()
        queries(t + 1, jnp.concatenate([wq[t, 0], wq[t, 1]], axis=1))
    fourth[0].wait_recv()
    far = lax.rem(z + 2, 4)
    handed.append(send(of_z(far, pl.ds(0, 1)), of_z(far, pl.ds(0, 1)), other))
    fourth[1].wait_recv()
    handed.append(send(of_z(far, pl.ds(1, 1)), of_z(far, pl.ds(1, 1)), other))
    fourth[2].wait_recv()
    far = lax.rem(y + 2, 4)
    handed.append(send(of_y(far, pl.ds(0, 2)), of_y(far, pl.ds(0, 2)), other))
    fourth[3].wait_recv()
    handed.append(send(of_y(far, pl.ds(2, 2)), of_y(far, pl.ds(2, 2)), other))
    out_half = w_out.at[pl.ds(pl.multiple_of(c * HEAD, HEAD), HEAD), :]
    out_got = [
        send(out_half, wo.at[t, c], peer) for t, peer in enumerate((beside, along, diagonal))
    ]
    handed_q[2].wait_recv()
    queries(3, jnp.concatenate([wq[2, 0], wq[2, 1]], axis=1))
    for copy in handed:
        copy.wait_recv()

    heads = QUERY_HEADS // KV_HEADS
    tall = heads * ROWS
    sub = 256
    for p in range(2):
        block = b if p == 0 else DEVS - 1 - b
        acc[...] = jnp.zeros_like(acc)
        top[...] = jnp.full_like(top, -1e30)

        def step(j, masked, p=p, block=block):
            k = buf[0, j // 4, j // 2 % 2, j % 2].reshape(CHUNK, HEAD)
            v = buf[1, j // 4, j // 2 % 2, j % 2].reshape(CHUNK, HEAD)
            ke = jnp.concatenate([k, k], axis=1)
            ve = jnp.concatenate([v, jnp.ones_like(v)], axis=1)
            for r in range(tall // sub):
                here = pl.ds(r * sub, sub)
                s = lax.dot_general(
                    qe[p, here, :], ke, (((1,), (1,)), ((), ())), preferred_element_type=f32
                )
                if masked:
                    row = lax.broadcasted_iota(jnp.int32, s.shape, 0) % ROWS + block * ROWS
                    col = lax.broadcasted_iota(jnp.int32, s.shape, 1) + j * CHUNK
                    s = jnp.where(col <= row, s, -1e30)
                old = top[here, :]
                new = jnp.maximum(old, jnp.max(s, axis=1, keepdims=True))
                top[here, :] = new
                weights = jnp.exp2(s - new[:, :1]).astype(bf16)
                fade = jnp.exp2(old - new)
                o = jnp.dot(weights, ve, preferred_element_type=f32)
                acc[here, :] = acc[here, :] * jnp.concatenate([fade, fade], axis=1) + o

        whole = block // (CHUNK // ROWS)

        def body(j, _, step=step):
            step(j, False)
            return 0

        lax.fori_loop(0, whole, body, 0)
        step(whole, True)
        for h in range(heads):
            here = pl.ds(h * ROWS, ROWS)
            attended[p * ROWS : (p + 1) * ROWS, h * HEAD : (h + 1) * HEAD] = (
                acc[here, :HEAD] / acc[here, HEAD:]
            ).astype(bf16)

    handed_o = []
    for t in range(3):
        out_got[t].wait_recv()
        handed_o.append(send(wo.at[t, c], wo.at[t, c], other))
    for copy in handed_o:
        copy.wait_recv()
    back = []
    wide = 512
    for n in range(WIDTH // wide):
        here = pl.ds(n * wide, wide)
        o = jnp.dot(attended[:, : 2 * HEAD], w_out[:, here], preferred_element_type=f32)
        for t in range(3):
            o = o + jnp.dot(
                attended[:, (t + 1) * 2 * HEAD : (t + 2) * 2 * HEAD],
                wo[t, :, :, here].reshape(2 * HEAD, wide),
                preferred_element_type=f32,
            )
        leaving[n] = o[ROWS:].astype(bf16)
        kept[:, here] = o[:ROWS]
        back.append(send(leaving.at[n], landing.at[n], partner))
    total = jnp.zeros((ROWS, 1), f32)
    for n in range(WIDTH // wide):
        here = pl.ds(n * wide, wide)
        back[n].wait_recv()
        r = tokens[:, here].astype(f32) + (kept[:, here] + landing[n].astype(f32))
        r = r.astype(bf16)
        residual[:, here] = r
        r = r.astype(f32)
        total = total + jnp.sum(r * r, axis=-1, keepdims=True)
    r = residual[...].astype(f32)
    normed2[...] = (r * lax.rsqrt(total * (1.0 / WIDTH) + EPS) * ln2[...]).astype(bf16)
    for copy in sent:
        copy.wait_send()


def before_experts(*args):
    f32, bf16 = jnp.float32, jnp.bfloat16
    vmem = pl.BlockSpec(memory_space=pltpu.VMEM)
    rows = QUERY_HEADS // KV_HEADS * ROWS
    made = jax.ShapeDtypeStruct((ROWS, WIDTH), bf16)
    copies = 64
    return pl.pallas_call(
        layer_kernel,
        out_shape=(made, made),
        in_specs=[vmem] * len(args),
        out_specs=(vmem, vmem),
        scratch_shapes=[
            pltpu.VMEM((2, ROWS, WIDTH), bf16),
            pltpu.VMEM((KV_HEADS, 2, ROWS, HEAD), bf16),
            pltpu.VMEM((2, 4, 2, 2, 4, 2, ROWS, HEAD), bf16),
            pltpu.VMEM((3, 2, WIDTH, HEAD), bf16),
            pltpu.VMEM((3, 2, HEAD, WIDTH), bf16),
            pltpu.VMEM((2, rows, 2 * HEAD), bf16),
            pltpu.VMEM((rows, 2 * HEAD), f32),
            pltpu.VMEM((rows, HEAD), f32),
            pltpu.VMEM((2 * ROWS, rows), bf16),
            pltpu.VMEM((4, ROWS, 512), bf16),
            pltpu.VMEM((4, ROWS, 512), bf16),
            pltpu.VMEM((ROWS, WIDTH), f32),
            pltpu.SemaphoreType.DMA((copies,)),
            pltpu.SemaphoreType.DMA((copies,)),
        ],
        compiler_params=pltpu.CompilerParams(
            collective_id=0, has_side_effects=True, vmem_limit_bytes=48 << 20
        ),
    )(*args)


GROUP = 16
STEP = 32


def sort_matrix(turned):
    r = lax.broadcasted_iota(jnp.int32, (256, 256), 1 if turned else 0)
    j = lax.broadcasted_iota(jnp.int32, (256, 256), 0 if turned else 1)
    same = (r // 64 == j // 4 % 4) & (r // 4 % 16 == j // 16) & (r % 4 == j % 4)
    return jnp.where(same, 1.0, 0.0).astype(jnp.bfloat16)


def expert_kernel(a_ref, wg_ref, wu_ref, wd_ref, o_ref, x_ref, y_ref):
    gather, spread = sort_matrix(False), sort_matrix(True)
    for h in range(STEP // GROUP):
        for k in range(3):
            part = a_ref[h * GROUP : (h + 1) * GROUP, 16 * k : 16 * k + 16, :].reshape(256, 512)
            part = jnp.dot(gather, part, preferred_element_type=jnp.float32).astype(jnp.bfloat16)
            first = (h * 3 + k) * 64
            for q in range(4):
                x_ref[first : first + 64, q * 512 : (q + 1) * 512] = part[q * 64 : (q + 1) * 64]
    x = x_ref[...]
    gate = jnp.dot(x, wg_ref[...], preferred_element_type=jnp.float32)
    up = jnp.dot(x, wu_ref[...], preferred_element_type=jnp.float32)
    hidden = (gate / (1.0 + jnp.exp(-gate)) * up).astype(jnp.bfloat16)
    y_ref[...] = jnp.dot(hidden, wd_ref[...], preferred_element_type=jnp.float32).astype(
        jnp.bfloat16
    )
    for h in range(STEP // GROUP):
        for k in range(3):
            first = (h * 3 + k) * 64
            part = jnp.concatenate(
                [y_ref[first : first + 64, q * 512 : (q + 1) * 512] for q in range(4)], axis=0
            )
            part = jnp.dot(spread, part, preferred_element_type=jnp.float32).astype(jnp.bfloat16)
            o_ref[h * GROUP : (h + 1) * GROUP, 16 * k : 16 * k + 16, :] = part.reshape(
                GROUP, 16, 512
            )


def experts(arrived, wg, wu, wd):
    rows = STEP * CAP
    once = pl.Buffered(1)
    return pl.pallas_call(
        expert_kernel,
        grid=(DEVS // STEP,),
        out_shape=jax.ShapeDtypeStruct(arrived.shape, jnp.bfloat16),
        in_specs=[
            pl.BlockSpec((STEP, 48, 512), lambda i: (i, 0, 0)),
            pl.BlockSpec((WIDTH, FF), lambda i: (0, 0), pipeline_mode=once),
            pl.BlockSpec((WIDTH, FF), lambda i: (0, 0), pipeline_mode=once),
            pl.BlockSpec((FF, WIDTH), lambda i: (0, 0), pipeline_mode=once),
        ],
        out_specs=pl.BlockSpec((STEP, 48, 512), lambda i: (i, 0, 0)),
        scratch_shapes=[
            pltpu.VMEM((rows, WIDTH), jnp.bfloat16),
            pltpu.VMEM((rows, WIDTH), jnp.bfloat16),
        ],
        compiler_params=pltpu.CompilerParams(vmem_limit_bytes=40 << 20),
        cost_estimate=pl.CostEstimate(
            flops=6 * DEVS * CAP * WIDTH * FF, bytes_accessed=22 << 20, transcendentals=0
        ),
    )(arrived, wg, wu, wd)


def shards(
    tokens,
    ln1_gain,
    w_query,
    key_weight,
    value_weight,
    q_gain,
    k_gain,
    w_out,
    ln2_gain,
    expert_ids,
    route_weights,
    w_gate,
    w_up,
    w_down,
):
    f32, bf16 = jnp.float32, jnp.bfloat16
    me = lax.axis_index("ctx") * 8 + lax.axis_index("exp")
    tables = [rope_tables(first * ROWS) for first in (me, DEVS - 1 - me)]
    cos = jnp.stack([jnp.concatenate([c, c], axis=1) for c, s in tables])
    sin = jnp.stack([jnp.concatenate([-s, s], axis=1) for c, s in tables])
    residual, normed2 = before_experts(
        tokens,
        ln1_gain.reshape(1, WIDTH),
        w_query,
        key_weight,
        value_weight,
        q_gain.reshape(1, HEAD),
        k_gain.reshape(1, HEAD),
        w_out,
        ln2_gain.reshape(1, WIDTH),
        cos,
        sin,
    )

    chosen = expert_ids[:, :, None] == jnp.arange(DEVS)[None, None, :]
    counts = jnp.any(chosen, axis=1)
    before = jnp.arange(ROWS)[:, None] > jnp.arange(ROWS)[None, :]
    rank = jnp.dot(before.astype(bf16), counts.astype(bf16), preferred_element_type=f32)
    slots = jnp.where(counts, rank, -1.0).T
    route = jnp.sum(
        jnp.where(chosen, (route_weights.astype(f32) / 1024.0)[:, :, None], 0.0), axis=1
    ).T
    row = jnp.arange(48)
    row_slot = (row // 16 * 4 + row % 4).astype(f32)
    row_part = row // 4 % 4
    hot = (jnp.tile(slots, (1, 4))[:, None, :] == row_slot[None, :, None]) & (
        row_part[None, :, None] == (jnp.arange(512) // ROWS)[None, None, :]
    )
    dispatch = hot.astype(bf16).reshape(DEVS * 48, 512)
    combine = (
        jnp.where(hot, jnp.tile(route, (1, 4))[:, None, :], 0.0)
        .astype(bf16)
        .reshape(DEVS * 48, 512)
    )
    parts = normed2.reshape(ROWS, 4, 512).transpose(1, 0, 2).reshape(512, 512)
    outgoing = jnp.dot(dispatch, parts, preferred_element_type=f32).astype(bf16)
    arrived = lax.all_to_all(outgoing, BOTH, split_axis=0, concat_axis=0, tiled=True)
    produced = experts(arrived.reshape(DEVS, 48, 512), w_gate[0], w_up[0], w_down[0])
    returned = lax.all_to_all(
        produced.reshape(DEVS * 48, 512), BOTH, split_axis=0, concat_axis=0, tiled=True
    )
    mixture = lax.dot_general(
        combine, returned, (((0,), (0,)), ((), ())), preferred_element_type=f32
    )
    mixture = mixture.reshape(4, ROWS, 512).transpose(1, 0, 2).reshape(ROWS, WIDTH)
    return (residual.astype(f32) + mixture).astype(bf16)


def solution(mesh):
    two = P(BOTH, None)
    three = P(BOTH, None, None)
    in_specs = (
        two,
        P(),
        P(None, "exp"),
        P(),
        P(),
        P(),
        P(),
        P("exp", None),
        P(),
        two,
        two,
        three,
        three,
        three,
    )
    return jax.shard_map(shards, mesh=mesh, in_specs=in_specs, out_specs=two, check_vma=False)
```

time: 382 us -> 316 us (0.83)
  waiting for transfers between devices: 85.1 us -> 59.9 us
  local copies, waits for them, and re-layouts: 42.5 us -> 18.8 us
  starting transfers between devices: 29 us -> 6.16 us
  Pallas kernels: 110 us -> 129 us
  matrix products: 19.3 us -> 11.3 us
  other arithmetic: 14.5 us -> 9.46 us
    ppermute x14 -> x0, waiting for transfers between devices: 25.1 us -> none  [the longest x1 13.4 us: shards(): theirs = lax.ppermute(theirs, BOTH, partner)]
    ppermute x14 -> x0, starting transfers between devices: 22.6 us -> none  [the longest x1 10 us: shards(): normed_partner = lax.ppermute(normed, BOTH, partner)]
    pallas_call x2 -> x1, Pallas kernels: 88.1 us -> 108 us  [before_experts(): pl.pallas_call(layer_kernel, out_shape=(made, made), in_specs=[vmem] * le...]
    unnamed x49 -> x29, local copies, waits for them, and re-layouts: 20.9 us -> 9.49 us
    dot_general x5 -> x0, matrix products: 8 us -> none  [the longest x2 5.87 us: queries_of(): q = jnp.dot(rows, weights, preferred_element_type=f32)]
    slice x1 -> x0, local copies, waits for them, and re-layouts: 6.02 us -> none  [shards(): attended = attend(blocks, queries, gathered[0], gathered[1])]
    dynamic_slice x2 -> x0, local copies, waits for them, and re-layouts: 3.91 us -> none  [the longest x1 2.03 us: shards(): q_half = lax.dynamic_slice_in_dim(w_query, core * HEAD, HEAD, 1)]
  transfers between devices with their start and end apart: 15 -> 1, of which waited for: 4 -> 1; matrix products, arithmetic and copies ran while one was open for 15% -> 5% of each run, Pallas kernels for 23% -> 0%
where the time goes in v2:
time: 316 us; the launch traced here: 315 us
  Pallas kernels  129 us (41%)
  blocking collectives  79.3 us (25%)
  waiting for transfers between devices  59.9 us (19%)
  local copies, waits for them, and re-layouts  18.8 us (6%)
  matrix products  11.3 us (4%)
  other arithmetic  9.46 us (3%)
  starting transfers between devices  6.16 us (2%)
    pallas_call x1, Pallas kernels, before_experts(): pl.pallas_call(layer_kernel, out_shape=(made, made), in_specs=[vmem] * le...  108 us
    all_to_all x1, blocking collectives, shards(): lax.all_to_all(outgoing, BOTH, split_axis=0, concat_axis=0, tiled=True)  79.3 us
    all_to_all x1, waiting for transfers between devices, shards(): lax.all_to_all(produced.reshape(DEVS * 48, 512), BOTH, split_axis=0, conc...  59.9 us
    pallas_call x1, Pallas kernels, experts(): pl.pallas_call(expert_kernel, grid=(DEVS // STEP,), out_shape=jax.ShapeDt...  21.6 us
    unnamed x29, local copies, waits for them, and re-layouts  9.49 us
    dot_general x1, local copies, waits for them, and re-layouts, shards(): lax.dot_general(combine, returned, (((0,), (0,)), ((), ())), preferred_el...  8.68 us
    dot_general x1, matrix products, shards(): lax.dot_general(combine, returned, (((0,), (0,)), ((), ())), preferred_el...  7.45 us
  transfers between devices with their start and end apart: 1, of which 1 were waited for; matrix products, arithmetic and copies ran while one was open for 5% of the time, Pallas kernels for 0%

profile of v2, /device:TPU:1, one launch (start us, length us, event | category | flops | bytes accessed | tf_op | source)
XLA Modules:
  0.0 314.6 jit_solution(5243932560408582488)
XLA Ops:
  0.1 0.8 copy.24
  0.9 0.3 fusion.2
  1.1 0.1 copy.25
  1.2 0.2 convolution_select_fusion
  1.5 0.5 fusion.4
  2.0 0.1 maximum_bitcast_fusion.2
  2.2 0.1 maximum_bitcast_fusion
  2.3 0.0 copy-start
  2.3 1.2 copy-done
  3.5 0.0 copy-start.1
  3.5 1.2 copy-done.1
  4.8 0.0 copy-start.2
  4.8 1.2 copy-done.2
  6.0 0.0 copy-start.3
  6.0 1.2 copy-done.3
  7.2 0.0 copy-start.4
  7.2 1.0 copy-done.4
  8.2 0.0 copy-start.5
  8.2 0.7 copy-done.5
  8.9 0.0 copy-start.6
  8.9 0.7 copy-done.6
  9.6 0.0 copy-start.7
  9.6 0.7 copy-done.7
  10.3 0.7 copy-done.8
  11.0 107.8 %shard_map.136 = (bf16[128,2048]{1,0:T(8,128)(2,1)S(1)}, bf16[128,2048]{1,0:T(8,128)(2,1)S(1)}) custom-call(bf16[128,2048]{1,0:T(8,128)(2,1)S(1)} %copy-done.4, f32[1,2048]{1,0:T(1,128)S(1)} %bitcast.61, bf16[2048,256]{1,0:T(8,128)(2,1)S(1)} %copy-done, bf16[2048,256]{1,0:T(8,128)(2,1)S(1)} %copy-done.1, bf16[2048,256]{1,0:T(8,128)(2,1)S(1)} %copy-done.2, ...), custom_call_target="tpu_custom_call" | custom-call | tf_op jit(solution)/shard_map/pallas_call | solution.py:308
  118.8 0.1 broadcast_compare_fusion
  118.9 2.1 compare_and_fusion
  121.0 3.7 %convolution_convert_fusion = bf16[6144,512]{1,0:T(8,128)(2,1)S(1)} fusion(pred[6144,512]{1,0:T(8,128)(4,1)S(1)} %bitcast.72, bf16[512,512]{1,0:T(8,128)(2,1)S(1)} %bitcast.78), kind=kOutput, calls=%fused_computation.5 | convolution fusion | flops 3224371200 | bytes 9961472 | tf_op jit(solution)/shard_map/dot_general | solution.py:455
  124.7 0.0 copy-start.9
  124.7 0.0 copy-start.10
  124.7 0.0 copy-start.11
  124.7 79.3 %all_to_all.18.a_ref = bf16[128,48,512]{2,1,0:T(8,128)(2,1)} all-to-all(bf16[128,48,512]{2,1,0:T(8,128)(2,1)S(1)} %bitcast.70), channel_id=1, replica_groups=mesh['ctx'=16,'exp'=8] {'ctx','exp'}, dimensions={0} | all-to-all | bytes 12582912 | tf_op jit(solution)/shard_map/all_to_all | solution.py:456
  204.0 0.0 copy-done.9
  204.0 0.0 copy-done.10
  204.0 0.0 copy-done.11
  204.0 21.6 %shard_map.137 = bf16[128,48,512]{2,1,0:T(8,128)(2,1)} custom-call(bf16[128,48,512]{2,1,0:T(8,128)(2,1)} %all_to_all.18.a_ref, bf16[2048,768]{1,0:T(8,128)(2,1)S(1)} %bitcast.65, bf16[2048,768]{1,0:T(8,128)(2,1)S(1)} %bitcast.66, bf16[768,2048]{1,0:T(8,128)(2,1)S(1)} %bitcast.67), custom_call_target="tpu_custom_call" | custom-call | flops 14495514624 | bytes 23068672 | tf_op jit(solution)/shard_map/pallas_call | solution.py:377
  225.6 6.2 %all-to-all-start.1 = ((bf16[128,48,512]{2,1,0:T(8,128)(2,1)}), bf16[128,48,512]{2,1,0:T(8,128)(2,1)}, u32[]{:S(2)}, u32[]{:S(2)}) async-start(bf16[128,48,512]{2,1,0:T(8,128)(2,1)} %shard_map.137), calls=%async_computation.1 | async-start | bytes 12582912 | tf_op jit(solution)/shard_map/all_to_all | solution.py:458
  231.8 0.0 copy-done.12
  231.8 0.1 copy.26
  231.9 0.4 select_reduce_fusion
  232.3 0.1 copy.27
  232.4 0.1 eq.78
  232.6 5.0 %fusion = bf16[6144,512]{1,0:T(8,128)(2,1)} fusion(bf16[128,512]{1,0:T(8,128)(2,1)S(1)} %bitcast.76, f32[6144]{0:T(1024)S(1)} %eq.78, f32[128,512]{1,0:T(8,128)S(1)} %bitcast.74, pred[48,512]{1,0:T(8,128)(4,1)S(1)} %broadcast_compare_fusion), kind=kLoop, calls=%fused_computation.1 | loop fusion | flops 9437184 | bytes 6733824 | tf_op jit(solution)/shard_map/convert_element_type | solution.py:451
  237.5 8.7 %copy.31 = bf16[512,6144]{1,0:T(8,128)(2,1)} copy(bf16[512,6144]{0,1:T(8,128)(2,1)} %bitcast.68) | data formatting | bytes 12582912 | tf_op jit(solution)/shard_map/dot_general | solution.py:461
  246.2 59.9 %all-to-all-done.1 = bf16[128,48,512]{2,1,0:T(8,128)(2,1)} async-done(((bf16[128,48,512]{2,1,0:T(8,128)(2,1)}), bf16[128,48,512]{2,1,0:T(8,128)(2,1)}, u32[]{:S(2)}, u32[]{:S(2)}) %all-to-all-start.1) | async-done | bytes 6291488 | tf_op jit(solution)/shard_map/all_to_all | solution.py:458
  306.1 7.5 %convolution_bitcast_fusion = f32[4,16,8,512]{3,2,1,0:T(8,128)S(1)} fusion(bf16[4,128,6144]{2,1,0:T(8,128)(2,1)} %bitcast.69, bf16[6144,512,1]{1,0,2:T(8,128)(2,1)} %bitcast.23), kind=kOutput, calls=%fused_computation.6 | convolution fusion | flops 3221225472 | bytes 13631488 | tf_op jit(solution)/shard_map/dot_general | solution.py:461
  313.6 0.1 copy.33
  313.7 0.9 add_convert_fusion
  (17 shorter events, 0.2 us)
Async XLA Ops:
  2.3 1.2 copy-start
  3.5 1.2 copy-start.1
  4.8 1.2 copy-start.2
  6.0 1.2 copy-start.3
  7.2 1.0 copy-start.4
  8.2 0.7 copy-start.5
  8.9 0.7 copy-start.6
  9.6 0.7 copy-start.7
  10.3 0.7 copy-start.8
  124.7 79.4 %copy-start.9 = (bf16[1,2048,768]{2,1,0:T(8,128)(2,1)S(1)}, bf16[1,2048,768]{2,1,0:T(8,128)(2,1)}, u32[]{:S(2)}) copy-start(bf16[1,2048,768]{2,1,0:T(8,128)(2,1)} %param.25) | copy-start | bytes 9437188
  124.7 79.3 %copy-start.10 = (bf16[1,2048,768]{2,1,0:T(8,128)(2,1)S(1)}, bf16[1,2048,768]{2,1,0:T(8,128)(2,1)}, u32[]{:S(2)}) copy-start(bf16[1,2048,768]{2,1,0:T(8,128)(2,1)} %param.26) | copy-start | bytes 9437188
  124.7 79.3 %copy-start.11 = (bf16[1,768,2048]{2,1,0:T(8,128)(2,1)S(1)}, bf16[1,768,2048]{2,1,0:T(8,128)(2,1)}, u32[]{:S(2)}) copy-start(bf16[1,768,2048]{2,1,0:T(8,128)(2,1)} %param.27) | copy-start | bytes 9437188
  225.6 6.2 %copy-start.12 = (s32[128,8]{0,1:T(8,128)S(1)}, s32[128,8]{0,1:T(8,128)}, u32[]{:S(2)}) copy-start(s32[128,8]{0,1:T(8,128)} %param.24) | copy-start | bytes 12292
  225.6 80.5 %all-to-all-start.1 = ((bf16[128,48,512]{2,1,0:T(8,128)(2,1)}), bf16[128,48,512]{2,1,0:T(8,128)(2,1)}, u32[]{:S(2)}, u32[]{:S(2)}) async-start(bf16[128,48,512]{2,1,0:T(8,128)(2,1)} %shard_map.137), calls=%async_computation.1 | async-start | bytes 12582912 | tf_op jit(solution)/shard_map/all_to_all | solution.py:458

commit v3 on v2

--- a/solution.py
+++ b/solution.py
@@ -8,8 +8,6 @@
 HEAD = 128
 KV_HEADS = 2
 QUERY_HEADS = 16
-TOP = 8
-CAP = 12
 ROWS = 128
 WIDTH = 2048
 FF = 768
@@ -332,68 +330,327 @@
     )(*args)
 
 
-GROUP = 16
-STEP = 32
-
-
-def sort_matrix(turned):
-    r = lax.broadcasted_iota(jnp.int32, (256, 256), 1 if turned else 0)
-    j = lax.broadcasted_iota(jnp.int32, (256, 256), 0 if turned else 1)
-    same = (r // 64 == j // 4 % 4) & (r // 4 % 16 == j // 16) & (r % 4 == j % 4)
+CUTS = ((0, 768), (768, 640), (1408, 640))
+ROUNDS = 3
+PLANE = 32
+ROUND_ROWS = 512
+
+
+def line_at(p, d, x, y, z, c):
+    if p == 0:
+        return x, y, (z + d) % 4, c
+    if p == 1:
+        return x, (y + d) % 4, z, c
+    return (x + d) % 4, y, z, c
+
+
+def plane_at(p, i, x, y, z, c):
+    a, b, dc = i % 4, i // 4 % 4, i // 16
+    if p == 0:
+        return (x + a) % 4, (y + b) % 4, z, (c + dc) % 2
+    if p == 1:
+        return (x + b) % 4, y, (z + a) % 4, (c + dc) % 2
+    return x, (y + a) % 4, (z + b) % 4, (c + dc) % 2
+
+
+def opposite(i):
+    return (4 - i % 4) % 4 + (4 - i // 4 % 4) % 4 * 4 + i // 16 * 16
+
+
+def reorder(p, turned):
+    shape = (ROUND_ROWS, ROUND_ROWS)
+    r = lax.broadcasted_iota(jnp.int32, shape, 1 if turned else 0)
+    j = lax.broadcasted_iota(jnp.int32, shape, 0 if turned else 1)
+    dz, dx, dy = r // 4 % 4, r // 16 % 4, r // 64 % 4
+    inner, low, high = (dy, dz, dx) if p == 1 else (dx, dy, dz)
+    same = j == r // 256 * 256 + high * 64 + low * 16 + inner * 4 + r % 4
     return jnp.where(same, 1.0, 0.0).astype(jnp.bfloat16)
 
 
-def expert_kernel(a_ref, wg_ref, wu_ref, wd_ref, o_ref, x_ref, y_ref):
-    gather, spread = sort_matrix(False), sort_matrix(True)
-    for h in range(STEP // GROUP):
-        for k in range(3):
-            part = a_ref[h * GROUP : (h + 1) * GROUP, 16 * k : 16 * k + 16, :].reshape(256, 512)
-            part = jnp.dot(gather, part, preferred_element_type=jnp.float32).astype(jnp.bfloat16)
-            first = (h * 3 + k) * 64
-            for q in range(4):
-                x_ref[first : first + 64, q * 512 : (q + 1) * 512] = part[q * 64 : (q + 1) * 64]
-    x = x_ref[...]
-    gate = jnp.dot(x, wg_ref[...], preferred_element_type=jnp.float32)
-    up = jnp.dot(x, wu_ref[...], preferred_element_type=jnp.float32)
-    hidden = (gate / (1.0 + jnp.exp(-gate)) * up).astype(jnp.bfloat16)
-    y_ref[...] = jnp.dot(hidden, wd_ref[...], preferred_element_type=jnp.float32).astype(
-        jnp.bfloat16
-    )
-    for h in range(STEP // GROUP):
-        for k in range(3):
-            first = (h * 3 + k) * 64
-            part = jnp.concatenate(
-                [y_ref[first : first + 64, q * 512 : (q + 1) * 512] for q in range(4)], axis=0
+def expert_kernel(
+    table,
+    rows,
+    residual,
+    w_gate,
+    w_up,
+    w_down,
+    out,
+    tables,
+    held0,
+    held1,
+    held2,
+    went0,
+    went1,
+    went2,
+    came0,
+    came1,
+    came2,
+    back0,
+    back1,
+    back2,
+    sums0,
+    sums1,
+    sums2,
+    gave0,
+    gave1,
+    gave2,
+    got0,
+    got1,
+    got2,
+    x_rows,
+    y_rows,
+    wg,
+    wu,
+    wd,
+    w_sem,
+    line_out,
+    line_in,
+    plane_out,
+    plane_in,
+):
+    f32, bf16 = jnp.float32, jnp.bfloat16
+    me = place()
+    held, went, came = (held0, held1, held2), (went0, went1, went2), (came0, came1, came2)
+    back, sums = (back0, back1, back2), (sums0, sums1, sums2)
+    gave, got = (gave0, gave1, gave2), (got0, got1, got2)
+
+    barrier = pltpu.get_barrier_semaphore()
+
+    def greet(i, _):
+        for p in range(3):
+            pl.semaphore_signal(
+                barrier, inc=1, device_id=ids(*plane_at(p, i, *me)), device_id_type=MESH
             )
-            part = jnp.dot(spread, part, preferred_element_type=jnp.float32).astype(jnp.bfloat16)
-            o_ref[h * GROUP : (h + 1) * GROUP, 16 * k : 16 * k + 16, :] = part.reshape(
-                GROUP, 16, 512
+        return 0
+
+    lax.fori_loop(1, PLANE, greet, 0)
+    loads = [
+        pltpu.make_async_copy(src, dst, w_sem.at[n])
+        for n, (src, dst) in enumerate(((w_gate, wg), (w_up, wu), (w_down, wd)))
+    ]
+    for load in loads:
+        load.start()
+    for p, (first, wide) in enumerate(CUTS):
+        held[p][0] = rows[:, first : first + wide]
+        tables[p, 0] = table[p, 0]
+    pl.semaphore_wait(barrier, 3 * (PLANE - 1))
+
+    def remote(src, dst, out_sem, in_sem, peer):
+        return pltpu.make_async_remote_copy(
+            src_ref=src,
+            dst_ref=dst,
+            send_sem=out_sem,
+            recv_sem=in_sem,
+            device_id=ids(*peer),
+            device_id_type=MESH,
+        )
+
+    lines = []
+    for d in range(1, 4):
+        for p, (first, wide) in enumerate(CUTS):
+            peer = line_at(p, 4 - d, *me)
+            for n, (src, dst) in enumerate(
+                (
+                    (table.at[p, d], tables.at[p, d]),
+                    (rows.at[:, pl.ds(first, wide)], held[p].at[d]),
+                )
+            ):
+                copy = remote(src, dst, line_out.at[n, p, d - 1], line_in.at[n, p, d - 1], peer)
+                copy.start()
+                lines.append(copy)
+    for copy in lines:
+        copy.wait_recv()
+
+    lane = lax.broadcasted_iota(jnp.int32, (16, 4 * ROWS), 1) // ROWS
+    line = lax.broadcasted_iota(jnp.int32, (16, 4 * ROWS), 0)
+    aim = jnp.where(lane == line // 4, line % 4, -100).astype(f32)
+
+    def wide_table(p, n):
+        t = jnp.concatenate([tables[p, d, n].astype(f32) for d in range(4)], axis=1)
+        return jnp.broadcast_to(t[:, None, :], (PLANE, 16, 4 * ROWS))
+
+    def hot(p, k):
+        return wide_table(p, 0) == (aim + 4.0 * k.astype(f32))[None]
+
+    def spread(way, k, src, dst):
+        def one(n, _):
+            i = n * 11 % PLANE
+            for p in range(3):
+                remote(
+                    src[p].at[k, i],
+                    dst[p].at[k, opposite(i)],
+                    plane_out.at[way, k, p],
+                    plane_in.at[way, k, p],
+                    plane_at(p, i, *me),
+                ).start()
+            return 0
+
+        lax.fori_loop(1, PLANE, one, 0)
+
+    def all_of(way, k, src, dst, p):
+        most = pl.ds(1, PLANE - 1)
+        return remote(
+            src[p].at[k, most],
+            dst[p].at[k, most],
+            plane_out.at[way, k, p],
+            plane_in.at[way, k, p],
+            plane_at(p, 1, *me),
+        )
+
+    def dispatch(k, _):
+        for p, (first, wide) in enumerate(CUTS):
+            picks = jnp.where(hot(p, k), 1.0, 0.0).astype(bf16).reshape(ROUND_ROWS, 4 * ROWS)
+            o = jnp.dot(
+                picks, held[p][...].reshape(4 * ROWS, wide), preferred_element_type=f32
+            ).astype(bf16)
+            went[p][k] = o.reshape(PLANE, 16, wide)
+            came[p][k, 0] = o[:16]
+        spread(0, k, went, came)
+        return 0
+
+    lax.fori_loop(0, ROUNDS, dispatch, 0)
+    for load in loads:
+        load.wait()
+
+    def expert(k, _):
+        for p, (first, wide) in enumerate(CUTS):
+            all_of(0, k, went, came, p).wait_recv()
+            part = came[p][k].reshape(ROUND_ROWS, wide)
+            if p:
+                part = jnp.dot(reorder(p, False), part, preferred_element_type=f32).astype(bf16)
+            x_rows[:, first : first + wide] = part
+        x = x_rows[...]
+        gate = jnp.dot(x, wg[...], preferred_element_type=f32)
+        up = jnp.dot(x, wu[...], preferred_element_type=f32)
+        hidden = (gate / (1.0 + jnp.exp(-gate)) * up).astype(bf16)
+        y_rows[...] = jnp.dot(hidden, wd[...], preferred_element_type=f32).astype(bf16)
+        for p, (first, wide) in enumerate(CUTS):
+            part = y_rows[:, first : first + wide]
+            if p:
+                part = jnp.dot(reorder(p, True), part, preferred_element_type=f32).astype(bf16)
+            all_of(0, k, went, came, p).wait_send()
+            went[p][k] = part.reshape(PLANE, 16, wide)
+            back[p][k, 0] = part[:16]
+        spread(1, k, went, back)
+        return 0
+
+    lax.fori_loop(0, ROUNDS, expert, 0)
+
+    for p in range(3):
+        sums[p][...] = jnp.zeros_like(sums[p])
+
+    def combine(k, _):
+        for p, (first, wide) in enumerate(CUTS):
+            weights = jnp.where(hot(p, k), wide_table(p, 1), 0.0)
+            weights = weights.astype(bf16).reshape(ROUND_ROWS, 4 * ROWS)
+            all_of(1, k, went, back, p).wait_recv()
+            sums[p][...] += lax.dot_general(
+                weights,
+                back[p][k].reshape(ROUND_ROWS, wide),
+                (((0,), (0,)), ((), ())),
+                preferred_element_type=f32,
             )
-
-
-def experts(arrived, wg, wu, wd):
-    rows = STEP * CAP
-    once = pl.Buffered(1)
+        return 0
+
+    lax.fori_loop(0, ROUNDS, combine, 0)
+    ends = []
+    for p in range(3):
+        for d in range(1, 4):
+            gave[p][d - 1] = sums[p][d * ROWS : (d + 1) * ROWS, :].astype(bf16)
+            copy = remote(
+                gave[p].at[d - 1],
+                got[p].at[d - 1],
+                line_out.at[2, p, d - 1],
+                line_in.at[2, p, d - 1],
+                line_at(p, d, *me),
+            )
+            copy.start()
+            ends.append(copy)
+    for p, (first, wide) in enumerate(CUTS):
+        total = sums[p][:ROWS, :]
+        for d in range(3):
+            ends[3 * p + d].wait_recv()
+            total = total + got[p][d].astype(f32)
+        out[:, first : first + wide] = (
+            residual[:, first : first + wide].astype(f32) + total
+        ).astype(bf16)
+    for copy in lines + ends:
+        copy.wait_send()
+
+    def finish(k, _):
+        for p in range(3):
+            all_of(1, k, went, back, p).wait_send()
+        return 0
+
+    lax.fori_loop(0, ROUNDS, finish, 0)
+
+
+def experts(table, rows, residual, w_gate, w_up, w_down):
+    f32, bf16 = jnp.float32, jnp.bfloat16
+    vmem = pl.BlockSpec(memory_space=pltpu.VMEM)
+    apart = pl.BlockSpec(memory_space=pl.ANY)
+
+    def parts(*front, dtype=bf16):
+        return [pltpu.VMEM((*front, wide), dtype) for _, wide in CUTS]
+
     return pl.pallas_call(
         expert_kernel,
-        grid=(DEVS // STEP,),
-        out_shape=jax.ShapeDtypeStruct(arrived.shape, jnp.bfloat16),
-        in_specs=[
-            pl.BlockSpec((STEP, 48, 512), lambda i: (i, 0, 0)),
-            pl.BlockSpec((WIDTH, FF), lambda i: (0, 0), pipeline_mode=once),
-            pl.BlockSpec((WIDTH, FF), lambda i: (0, 0), pipeline_mode=once),
-            pl.BlockSpec((FF, WIDTH), lambda i: (0, 0), pipeline_mode=once),
+        out_shape=jax.ShapeDtypeStruct((ROWS, WIDTH), bf16),
+        in_specs=[vmem, vmem, vmem, apart, apart, apart],
+        out_specs=vmem,
+        scratch_shapes=[
+            pltpu.VMEM((3, 4, 2, PLANE, ROWS), bf16),
+            *parts(4, ROWS),
+            *parts(ROUNDS, PLANE, 16),
+            *parts(ROUNDS, PLANE, 16),
+            *parts(ROUNDS, PLANE, 16),
+            *parts(4 * ROWS, dtype=f32),
+            *parts(3, ROWS),
+            *parts(3, ROWS),
+            pltpu.VMEM((ROUND_ROWS, WIDTH), bf16),
+            pltpu.VMEM((ROUND_ROWS, WIDTH), bf16),
+            pltpu.VMEM((WIDTH, FF), bf16),
+            pltpu.VMEM((WIDTH, FF), bf16),
+            pltpu.VMEM((FF, WIDTH), bf16),
+            pltpu.SemaphoreType.DMA((3,)),
+            pltpu.SemaphoreType.DMA((3, 3, 3)),
+            pltpu.SemaphoreType.DMA((3, 3, 3)),
+            pltpu.SemaphoreType.DMA((2, ROUNDS, 3)),
+            pltpu.SemaphoreType.DMA((2, ROUNDS, 3)),
         ],
-        out_specs=pl.BlockSpec((STEP, 48, 512), lambda i: (i, 0, 0)),
-        scratch_shapes=[
-            pltpu.VMEM((rows, WIDTH), jnp.bfloat16),
-            pltpu.VMEM((rows, WIDTH), jnp.bfloat16),
-        ],
-        compiler_params=pltpu.CompilerParams(vmem_limit_bytes=40 << 20),
-        cost_estimate=pl.CostEstimate(
-            flops=6 * DEVS * CAP * WIDTH * FF, bytes_accessed=22 << 20, transcendentals=0
+        compiler_params=pltpu.CompilerParams(
+            collective_id=1, has_side_effects=True, vmem_limit_bytes=58 << 20
         ),
-    )(arrived, wg, wu, wd)
+    )(table, rows, residual, w_gate, w_up, w_down)
+
+
+def expert_table(expert_ids, route_weights):
+    f32, bf16 = jnp.float32, jnp.bfloat16
+    chosen = expert_ids[:, :, None] == jnp.arange(DEVS)[None, None, :]
+    counts = jnp.any(chosen, axis=1)
+    before = jnp.arange(ROWS)[:, None] > jnp.arange(ROWS)[None, :]
+    rank = jnp.dot(before.astype(bf16), counts.astype(bf16), preferred_element_type=f32)
+    slots = jnp.where(counts, rank, -1.0)
+    route = jnp.sum(
+        jnp.where(chosen, (route_weights.astype(f32) / 1024.0)[:, :, None], 0.0), axis=1
+    )
+    i = jnp.arange(PLANE)
+    wanted = []
+    for p in range(3):
+        for d in range(4):
+            x, y, z, c = plane_at(p, i, *line_at(p, 4 - d, *place()))
+            context, expert = ids(x, y, z, c)
+            wanted.append(context * 8 + expert + 0 * i)
+    picks = (jnp.concatenate(wanted)[:, None] == jnp.arange(DEVS)[None, :]).astype(bf16)
+    table = jnp.stack(
+        [
+            lax.dot_general(
+                picks, v.astype(bf16), (((1,), (1,)), ((), ())), preferred_element_type=f32
+            )
+            for v in (slots, route)
+        ]
+    ).astype(bf16)
+    return table.reshape(2, 3, 4, PLANE, ROWS).transpose(1, 2, 0, 3, 4)
 
 
 def shards(
@@ -412,7 +669,6 @@
     w_up,
     w_down,
 ):
-    f32, bf16 = jnp.float32, jnp.bfloat16
     me = lax.axis_index("ctx") * 8 + lax.axis_index("exp")
     tables = [rope_tables(first * ROWS) for first in (me, DEVS - 1 - me)]
     cos = jnp.stack([jnp.concatenate([c, c], axis=1) for c, s in tables])
@@ -431,38 +687,8 @@
         sin,
     )
 
-    chosen = expert_ids[:, :, None] == jnp.arange(DEVS)[None, None, :]
-    counts = jnp.any(chosen, axis=1)
-    before = jnp.arange(ROWS)[:, None] > jnp.arange(ROWS)[None, :]
-    rank = jnp.dot(before.astype(bf16), counts.astype(bf16), preferred_element_type=f32)
-    slots = jnp.where(counts, rank, -1.0).T
-    route = jnp.sum(
-        jnp.where(chosen, (route_weights.astype(f32) / 1024.0)[:, :, None], 0.0), axis=1
-    ).T
-    row = jnp.arange(48)
-    row_slot = (row // 16 * 4 + row % 4).astype(f32)
-    row_part = row // 4 % 4
-    hot = (jnp.tile(slots, (1, 4))[:, None, :] == row_slot[None, :, None]) & (
-        row_part[None, :, None] == (jnp.arange(512) // ROWS)[None, None, :]
-    )
-    dispatch = hot.astype(bf16).reshape(DEVS * 48, 512)
-    combine = (
-        jnp.where(hot, jnp.tile(route, (1, 4))[:, None, :], 0.0)
-        .astype(bf16)
-        .reshape(DEVS * 48, 512)
-    )
-    parts = normed2.reshape(ROWS, 4, 512).transpose(1, 0, 2).reshape(512, 512)
-    outgoing = jnp.dot(dispatch, parts, preferred_element_type=f32).astype(bf16)
-    arrived = lax.all_to_all(outgoing, BOTH, split_axis=0, concat_axis=0, tiled=True)
-    produced = experts(arrived.reshape(DEVS, 48, 512), w_gate[0], w_up[0], w_down[0])
-    returned = lax.all_to_all(
-        produced.reshape(DEVS * 48, 512), BOTH, split_axis=0, concat_axis=0, tiled=True
-    )
-    mixture = lax.dot_general(
-        combine, returned, (((0,), (0,)), ((), ())), preferred_element_type=f32
-    )
-    mixture = mixture.reshape(4, ROWS, 512).transpose(1, 0, 2).reshape(ROWS, WIDTH)
-    return (residual.astype(f32) + mixture).astype(bf16)
+    table = expert_table(expert_ids, route_weights)
+    return experts(table, normed2, residual, w_gate[0], w_up[0], w_down[0])
 
 
 def solution(mesh):

time: 316 us -> 250 us (0.79)
  Pallas kernels: 129 us -> 238 us
  blocking collectives: 79.3 us -> 0 us
  waiting for transfers between devices: 59.9 us -> 0 us
  local copies, waits for them, and re-layouts: 18.8 us -> 6.72 us
  matrix products: 11.3 us -> 0.56 us
  other arithmetic: 9.46 us -> 3.24 us
  starting transfers between devices: 6.16 us -> 0 us
    pallas_call x1, Pallas kernels: 21.6 us -> 129 us  [experts(): pl.pallas_call(expert_kernel, out_shape=jax.ShapeDtypeStruct((ROWS, WIDTH...]
    all_to_all x1 -> x0, blocking collectives: 79.3 us -> none  [shards(): lax.all_to_all(outgoing, BOTH, split_axis=0, concat_axis=0, tiled=True)]
    all_to_all x1 -> x0, waiting for transfers between devices: 59.9 us -> none  [shards(): lax.all_to_all(produced.reshape(DEVS * 48, 512), BOTH, split_axis=0, conc...]
    dot_general x3 -> x2, matrix products: 11.3 us -> 0.56 us  [expert_table(): lax.dot_general(picks, v.astype(bf16), (((1,), (1,)), ((), ())), preferre...]
    dot_general x1 -> x0, local copies, waits for them, and re-layouts: 8.68 us -> none  [shards(): lax.dot_general(combine, returned, (((0,), (0,)), ((), ())), preferred_el...]
    all_to_all x1 -> x0, starting transfers between devices: 6.16 us -> none  [shards(): lax.all_to_all(produced.reshape(DEVS * 48, 512), BOTH, split_axis=0, conc...]
    convert_element_type x3 -> x0, other arithmetic: 5.87 us -> none  [the longest x1 4.97 us: shards(): combine = jnp.where(hot, jnp.tile(route, (1, 4))[:, None, :], 0.0).astype...]
    unnamed x29 -> x24, local copies, waits for them, and re-layouts: 9.49 us -> 6.53 us
  transfers between devices with their start and end apart: 1 -> 0, of which waited for: 1 -> 0; matrix products, arithmetic and copies ran while one was open for 5% -> 0% of each run, Pallas kernels for 0% -> 0%
where the time goes in v3:
time: 250 us; the launch traced here: 249 us
  Pallas kernels  238 us (95%)
  local copies, waits for them, and re-layouts  6.72 us (3%)
  other arithmetic  3.24 us (1%)
    pallas_call x1, Pallas kernels, experts(): pl.pallas_call(expert_kernel, out_shape=jax.ShapeDtypeStruct((ROWS, WIDTH...  129 us
    pallas_call x1, Pallas kernels, before_experts(): pl.pallas_call(layer_kernel, out_shape=(made, made), in_specs=[vmem] * le...  109 us
    unnamed x24, local copies, waits for them, and re-layouts  6.53 us

profile of v3, /device:TPU:1, one launch (start us, length us, event | category | flops | bytes accessed | tf_op | source)
XLA Modules:
  0.0 249.3 jit_solution(7663442011629294950)
XLA Ops:
  0.0 0.0 copy-start.8
  0.0 0.0 copy-start.10
  0.0 0.0 copy-start.9
  0.0 0.0 copy-start.2
  0.0 0.0 copy-start.1
  0.0 0.0 copy-start
  0.0 0.0 copy-start.7
  0.6 0.1 concatenate.17
  0.7 1.0 convert_multiply_fusion
  1.7 0.1 copy.18
  1.8 0.8 copy.17
  2.6 0.4 select_reduce_fusion
  3.0 0.3 fusion.1
  3.2 0.2 convolution_convert_fusion
  3.5 0.3 convolution_convert_fusion.1
  3.8 0.7 maximum_bitcast_fusion.table
  4.5 0.5 fusion.6
  5.0 0.1 maximum_bitcast_fusion.3
  5.2 0.1 maximum_bitcast_fusion.1
  5.3 0.0 copy-done.8
  5.3 0.0 copy-done.10
  5.3 0.0 copy-done.9
  5.3 0.0 copy-done.2
  5.3 0.0 copy-done.1
  5.3 0.0 copy-done
  5.3 0.0 copy-done.7
  5.4 0.0 copy-start.3
  5.4 1.2 copy-done.3
  6.6 0.0 copy-start.6
  6.6 1.0 copy-done.6
  7.6 109.0 %shard_map.136 = (bf16[128,2048]{1,0:T(8,128)(2,1)S(1)}, bf16[128,2048]{1,0:T(8,128)(2,1)S(1)}) custom-call(bf16[128,2048]{1,0:T(8,128)(2,1)S(1)} %copy-done.6, f32[1,2048]{1,0:T(1,128)S(1)} %bitcast.21, bf16[2048,256]{1,0:T(8,128)(2,1)S(1)} %copy-done, bf16[2048,256]{1,0:T(8,128)(2,1)S(1)} %copy-done.1, bf16[2048,256]{1,0:T(8,128)(2,1)S(1)} %copy-done.2, ...), custom_call_target="tpu_custom_call" | custom-call | tf_op jit(solution)/shard_map/pallas_call | solution.py:306
  116.6 0.0 copy-start.4
  116.7 0.8 copy-done.4
  117.4 0.0 copy-start.5
  117.4 0.8 copy-done.5
  118.2 129.2 %shard_map.137 = bf16[128,2048]{1,0:T(8,128)(2,1)} custom-call(bf16[3,4,2,32,128]{4,3,2,1,0:T(8,128)(2,1)} %maximum_bitcast_fusion.table, bf16[128,2048]{1,0:T(8,128)(2,1)} %copy-done.5, bf16[128,2048]{1,0:T(8,128)(2,1)} %copy-done.4, bf16[2048,768]{1,0:T(8,128)(2,1)} %bitcast.25, bf16[2048,768]{1,0:T(8,128)(2,1)} %bitcast.26, bf16[768,2048]{1,0:T(8,128)(2,1)} %bitcast.27), custom_call_target="tpu_custom_call" | custom-call | tf_op jit(solution)/shard_map/pallas_call | solution.py:596
  247.4 1.9 copy.20
  (11 shorter events, 0.2 us)
Async XLA Ops:
  0.0 5.3 %copy-start.8 = (f32[2048]{0:T(1024)S(1)}, f32[2048]{0:T(1024)}, u32[]{:S(2)}) copy-start(f32[2048]{0:T(1024)} %param.22) | copy-start | bytes 24580
  0.0 5.3 %copy-start.10 = (f32[128]{0:T(128)S(1)}, f32[128]{0:T(128)}, u32[]{:S(2)}) copy-start(f32[128]{0:T(128)} %param.20) | copy-start | bytes 1540
  0.0 5.3 %copy-start.9 = (f32[128]{0:T(128)S(1)}, f32[128]{0:T(128)}, u32[]{:S(2)}) copy-start(f32[128]{0:T(128)} %param.19) | copy-start | bytes 1540
  0.0 5.3 %copy-start.2 = (bf16[2048,256]{1,0:T(8,128)(2,1)S(1)}, bf16[2048,256]{1,0:T(8,128)(2,1)}, u32[]{:S(2)}) copy-start(bf16[2048,256]{1,0:T(8,128)(2,1)} %w_value.1) | copy-start | bytes 3145732
  0.0 5.3 %copy-start.1 = (bf16[2048,256]{1,0:T(8,128)(2,1)S(1)}, bf16[2048,256]{1,0:T(8,128)(2,1)}, u32[]{:S(2)}) copy-start(bf16[2048,256]{1,0:T(8,128)(2,1)} %w_key.1) | copy-start | bytes 3145732
  0.0 5.3 %copy-start = (bf16[2048,256]{1,0:T(8,128)(2,1)S(1)}, bf16[2048,256]{1,0:T(8,128)(2,1)}, u32[]{:S(2)}) copy-start(bf16[2048,256]{1,0:T(8,128)(2,1)} %w_query.1) | copy-start | bytes 3145732
  0.0 5.3 %copy-start.7 = (f32[2048]{0:T(1024)S(1)}, f32[2048]{0:T(1024)}, u32[]{:S(2)}) copy-start(f32[2048]{0:T(1024)} %param.15) | copy-start | bytes 24580
  5.4 1.2 copy-start.3
  6.6 1.0 copy-start.6
  116.6 0.8 copy-start.4
  117.4 0.8 copy-start.5

commit v4 on v3

--- a/solution.py
+++ b/solution.py
@@ -8,6 +8,7 @@
 HEAD = 128
 KV_HEADS = 2
 QUERY_HEADS = 16
+TOP = 8
 ROWS = 128
 WIDTH = 2048
 FF = 768
@@ -36,6 +37,35 @@
     return ((z * 2 + y // 2) * 2 + core, x * 2 + y % 2)
 
 
+def expert_table(named, route, me):
+    f32, bf16 = jnp.float32, jnp.bfloat16
+    square = (DEVS, ROWS)
+    expert = lax.broadcasted_iota(jnp.int32, square, 0)
+    counts, weights = jnp.zeros(square, f32), jnp.zeros(square, f32)
+    for k in range(TOP):
+        chosen = named[k : k + 1, :] == expert
+        counts = jnp.where(chosen, 1.0, counts)
+        weights = jnp.where(chosen, route[k : k + 1, :].astype(f32) * (1.0 / 1024.0), weights)
+    before = expert < lax.broadcasted_iota(jnp.int32, square, 1)
+    rank = jnp.dot(
+        counts.astype(bf16), jnp.where(before, 1.0, 0.0).astype(bf16), preferred_element_type=f32
+    )
+    slots = jnp.where(counts > 0.0, rank, -1.0).astype(bf16)
+    shape = (PLANE, DEVS)
+    i, column = lax.broadcasted_iota(jnp.int32, shape, 0), lax.broadcasted_iota(jnp.int32, shape, 1)
+    picks = []
+    for p in range(3):
+        for d in range(4):
+            context, place_in = ids(*plane_at(p, i, *line_at(p, 4 - d, *me)))
+            picks.append(jnp.where(column == context * 8 + place_in, 1.0, 0.0))
+    picks = jnp.concatenate(picks, axis=0).astype(bf16)
+    both = [
+        jnp.dot(picks, v, preferred_element_type=f32).astype(bf16)
+        for v in (slots, weights.astype(bf16))
+    ]
+    return jnp.stack([v.reshape(12, PLANE, ROWS) for v in both], axis=1)
+
+
 def norm_rows(v, gain):
     return v * lax.rsqrt(jnp.mean(v * v, axis=-1, keepdims=True) + EPS) * gain
 
@@ -47,17 +77,24 @@
 def layer_kernel(
     tokens,
     ln1,
+    far_query,
+    far_key,
+    far_value,
+    q_gain,
+    k_gain,
+    far_out,
+    ln2,
+    cos,
+    sin,
+    named,
+    route,
+    residual,
+    normed2,
+    table,
     w_query,
     w_key,
     w_value,
-    q_gain,
-    k_gain,
     w_out,
-    ln2,
-    cos,
-    sin,
-    residual,
-    normed2,
     normed,
     own,
     buf,
@@ -70,6 +107,7 @@
     leaving,
     landing,
     kept,
+    load_sem,
     out_sem,
     in_sem,
 ):
@@ -92,6 +130,12 @@
     for peer in peers:
         pl.semaphore_signal(barrier, inc=1, device_id=peer, device_id_type=MESH)
 
+    pairs = ((far_key, w_key), (far_value, w_value), (far_query, w_query), (far_out, w_out))
+    loads = [
+        pltpu.make_async_copy(src, dst, load_sem.at[n]) for n, (src, dst) in enumerate(pairs)
+    ]
+    for load in loads:
+        load.start()
     sent = []
 
     def send(src, dst, peer):
@@ -109,6 +153,13 @@
 
     rows = norm_rows(tokens[...].astype(f32), ln1[...]).astype(bf16)
     normed[0] = rows
+    pl.semaphore_wait(barrier, len(peers))
+    half = far_query.at[:, pl.ds(pl.multiple_of(c * HEAD, HEAD), HEAD)]
+    q1 = send(half, wq.at[0, c], beside)
+    q2 = send(half, wq.at[1, c], along)
+    swap = send(normed.at[0], normed.at[1], partner)
+    loads[0].wait()
+    loads[1].wait()
     keys = jnp.dot(rows, w_key[...], preferred_element_type=f32)
     values = jnp.dot(rows, w_value[...], preferred_element_type=f32).astype(bf16)
     for g in range(KV_HEADS):
@@ -116,17 +167,12 @@
         own[g, 0] = turn(k, cos[0], sin[0]).astype(bf16)
         own[g, 1] = values[:, g * HEAD : (g + 1) * HEAD]
     buf[c, z, yh, c, x, yl] = own[x // 2, c]
-    pl.semaphore_wait(barrier, len(peers))
-
     first = []
     for px, pc in near[1:]:
         first.append(
             send(own.at[px // 2, pc], buf.at[pc, z, yh, c, x, yl], ids(px, y, z, pc))
         )
-    half = w_query.at[:, pl.ds(pl.multiple_of(c * HEAD, HEAD), HEAD)]
-    q1 = send(half, wq.at[0, c], beside)
-    q2 = send(half, wq.at[1, c], along)
-    swap = send(normed.at[0], normed.at[1], partner)
+    table[...] = expert_table(named[...], route[...], (x, y, z, c)).reshape(table.shape)
     for copy in first:
         copy.wait_recv()
 
@@ -192,13 +238,86 @@
                 qe[p, here, :HEAD] = v_hi
                 qe[p, here, HEAD:] = (v - v_hi.astype(f32)).astype(bf16)
 
+    out_half = far_out.at[pl.ds(pl.multiple_of(c * HEAD, HEAD), HEAD), :]
+    o1 = send(out_half, wo.at[0, c], beside)
+    o2 = send(out_half, wo.at[1, c], along)
+    loads[2].wait()
+    loads[3].wait()
     swap.wait_recv()
     queries(0, w_query[...])
     q3.wait_recv()
     handed_q.append(send(wq.at[2, c], wq.at[2, c], other))
-    for t in range(2):
+    for t in range(3):
         handed_q[t].wait_recv()
         queries(t + 1, jnp.concatenate([wq[t, 0], wq[t, 1]], axis=1))
+
+    heads = QUERY_HEADS // KV_HEADS
+    tall = heads * ROWS
+    sub = 256
+    acc[...] = jnp.zeros_like(acc)
+    top[...] = jnp.full_like(top, -1e30)
+
+    def step(p, block, jz, jy, high_half, base, masked):
+        part = pl.ds(2 * high_half, 2)
+        k = buf[0, jz, jy, :, part].reshape(CHUNK, HEAD)
+        v = buf[1, jz, jy, :, part].reshape(CHUNK, HEAD)
+        ke = jnp.concatenate([k, k], axis=1)
+        ve = jnp.concatenate([v, jnp.ones_like(v)], axis=1)
+        scores = [
+            lax.dot_general(
+                qe[p, pl.ds(r * sub, sub), :],
+                ke,
+                (((1,), (1,)), ((), ())),
+                preferred_element_type=f32,
+            )
+            for r in range(tall // sub)
+        ]
+        for r, s in enumerate(scores):
+            here = pl.ds(r * sub, sub)
+            if masked:
+                row = lax.broadcasted_iota(jnp.int32, s.shape, 0) % ROWS + block * ROWS
+                col = lax.broadcasted_iota(jnp.int32, s.shape, 1)
+                col = col + col // (CHUNK // 2) * (CHUNK // 2) + base * ROWS
+                s = jnp.where(col <= row, s, -1e30)
+            old = top[p, here, :]
+            new = jnp.maximum(old, jnp.max(s, axis=1, keepdims=True))
+            top[p, here, :] = new
+            weights = jnp.exp2(s - new[:, :1]).astype(bf16)
+            fade = jnp.exp2(old - new)
+            o = jnp.dot(weights, ve, preferred_element_type=f32)
+            acc[p, here, :] = acc[p, here, :] * jnp.concatenate([fade, fade], axis=1) + o
+
+    def chunks(first_chunk, last_chunk, find):
+        def body(n, _):
+            p = n % 2
+            jz, jy, high_half = find(n // 2)
+            block = b + p * (DEVS - 1 - 2 * b)
+            base = (jz * 2 + jy) * 16 + high_half * 4
+
+            @pl.when(base + 11 < block)
+            def _():
+                step(p, block, jz, jy, high_half, base, False)
+
+            @pl.when((base <= block) & (base + 11 >= block))
+            def _():
+                step(p, block, jz, jy, high_half, base, True)
+
+            return 0
+
+        lax.fori_loop(2 * first_chunk, 2 * last_chunk, body, 0)
+
+    def early(m):
+        late = m // 6
+        jz = (1 - late) * ((z + 3 + m // 2) % 4) + late * (m - 6)
+        return jz, (1 - late) * (m % 2) + late * yh, late
+
+    def later(m):
+        late = (m + 4) // 6
+        return (1 - late) * ((z + 2) % 4) + late * (m - 2), (1 - late) * m + late * (1 - yh), late
+
+    for copy in handed[:6]:
+        copy.wait_recv()
+    chunks(0, 5, early)
     fourth[0].wait_recv()
     far = lax.rem(z + 2, 4)
     handed.append(send(of_z(far, pl.ds(0, 1)), of_z(far, pl.ds(0, 1)), other))
@@ -209,63 +328,23 @@
     handed.append(send(of_y(far, pl.ds(0, 2)), of_y(far, pl.ds(0, 2)), other))
     fourth[3].wait_recv()
     handed.append(send(of_y(far, pl.ds(2, 2)), of_y(far, pl.ds(2, 2)), other))
-    out_half = w_out.at[pl.ds(pl.multiple_of(c * HEAD, HEAD), HEAD), :]
-    out_got = [
-        send(out_half, wo.at[t, c], peer) for t, peer in enumerate((beside, along, diagonal))
-    ]
-    handed_q[2].wait_recv()
-    queries(3, jnp.concatenate([wq[2, 0], wq[2, 1]], axis=1))
-    for copy in handed:
+    o1.wait_recv()
+    o3 = send(wo.at[0, c], wo.at[2, c], along)
+    handed_o = [send(wo.at[0, c], wo.at[0, c], other)]
+    chunks(5, 10, early)
+    o2.wait_recv()
+    handed_o.append(send(wo.at[1, c], wo.at[1, c], other))
+    for copy in handed[6:]:
         copy.wait_recv()
-
-    heads = QUERY_HEADS // KV_HEADS
-    tall = heads * ROWS
-    sub = 256
+    chunks(0, 6, later)
     for p in range(2):
-        block = b if p == 0 else DEVS - 1 - b
-        acc[...] = jnp.zeros_like(acc)
-        top[...] = jnp.full_like(top, -1e30)
-
-        def step(j, masked, p=p, block=block):
-            k = buf[0, j // 4, j // 2 % 2, j % 2].reshape(CHUNK, HEAD)
-            v = buf[1, j // 4, j // 2 % 2, j % 2].reshape(CHUNK, HEAD)
-            ke = jnp.concatenate([k, k], axis=1)
-            ve = jnp.concatenate([v, jnp.ones_like(v)], axis=1)
-            for r in range(tall // sub):
-                here = pl.ds(r * sub, sub)
-                s = lax.dot_general(
-                    qe[p, here, :], ke, (((1,), (1,)), ((), ())), preferred_element_type=f32
-                )
-                if masked:
-                    row = lax.broadcasted_iota(jnp.int32, s.shape, 0) % ROWS + block * ROWS
-                    col = lax.broadcasted_iota(jnp.int32, s.shape, 1) + j * CHUNK
-                    s = jnp.where(col <= row, s, -1e30)
-                old = top[here, :]
-                new = jnp.maximum(old, jnp.max(s, axis=1, keepdims=True))
-                top[here, :] = new
-                weights = jnp.exp2(s - new[:, :1]).astype(bf16)
-                fade = jnp.exp2(old - new)
-                o = jnp.dot(weights, ve, preferred_element_type=f32)
-                acc[here, :] = acc[here, :] * jnp.concatenate([fade, fade], axis=1) + o
-
-        whole = block // (CHUNK // ROWS)
-
-        def body(j, _, step=step):
-            step(j, False)
-            return 0
-
-        lax.fori_loop(0, whole, body, 0)
-        step(whole, True)
         for h in range(heads):
             here = pl.ds(h * ROWS, ROWS)
             attended[p * ROWS : (p + 1) * ROWS, h * HEAD : (h + 1) * HEAD] = (
-                acc[here, :HEAD] / acc[here, HEAD:]
+                acc[p, here, :HEAD] / acc[p, here, HEAD:]
             ).astype(bf16)
-
-    handed_o = []
-    for t in range(3):
-        out_got[t].wait_recv()
-        handed_o.append(send(wo.at[t, c], wo.at[t, c], other))
+    o3.wait_recv()
+    handed_o.append(send(wo.at[2, c], wo.at[2, c], other))
     for copy in handed_o:
         copy.wait_recv()
     back = []
@@ -300,32 +379,38 @@
 def before_experts(*args):
     f32, bf16 = jnp.float32, jnp.bfloat16
     vmem = pl.BlockSpec(memory_space=pltpu.VMEM)
+    apart = pl.BlockSpec(memory_space=pl.ANY)
     rows = QUERY_HEADS // KV_HEADS * ROWS
     made = jax.ShapeDtypeStruct((ROWS, WIDTH), bf16)
     copies = 64
     return pl.pallas_call(
         layer_kernel,
-        out_shape=(made, made),
-        in_specs=[vmem] * len(args),
-        out_specs=(vmem, vmem),
+        out_shape=(made, made, jax.ShapeDtypeStruct((3, 4, 2, PLANE, ROWS), bf16)),
+        in_specs=[apart if n in (2, 3, 4, 7) else vmem for n in range(len(args))],
+        out_specs=(vmem, vmem, vmem),
         scratch_shapes=[
+            pltpu.VMEM((WIDTH, 2 * HEAD), bf16),
+            pltpu.VMEM((WIDTH, 2 * HEAD), bf16),
+            pltpu.VMEM((WIDTH, 2 * HEAD), bf16),
+            pltpu.VMEM((2 * HEAD, WIDTH), bf16),
             pltpu.VMEM((2, ROWS, WIDTH), bf16),
             pltpu.VMEM((KV_HEADS, 2, ROWS, HEAD), bf16),
             pltpu.VMEM((2, 4, 2, 2, 4, 2, ROWS, HEAD), bf16),
             pltpu.VMEM((3, 2, WIDTH, HEAD), bf16),
             pltpu.VMEM((3, 2, HEAD, WIDTH), bf16),
             pltpu.VMEM((2, rows, 2 * HEAD), bf16),
-            pltpu.VMEM((rows, 2 * HEAD), f32),
-            pltpu.VMEM((rows, HEAD), f32),
+            pltpu.VMEM((2, rows, 2 * HEAD), f32),
+            pltpu.VMEM((2, rows, HEAD), f32),
             pltpu.VMEM((2 * ROWS, rows), bf16),
             pltpu.VMEM((4, ROWS, 512), bf16),
             pltpu.VMEM((4, ROWS, 512), bf16),
             pltpu.VMEM((ROWS, WIDTH), f32),
+            pltpu.SemaphoreType.DMA((4,)),
             pltpu.SemaphoreType.DMA((copies,)),
             pltpu.SemaphoreType.DMA((copies,)),
         ],
         compiler_params=pltpu.CompilerParams(
-            collective_id=0, has_side_effects=True, vmem_limit_bytes=48 << 20
+            collective_id=0, has_side_effects=True, vmem_limit_bytes=60 << 20
         ),
     )(*args)
 
@@ -370,7 +455,6 @@
 def expert_kernel(
     table,
     rows,
-    residual,
     w_gate,
     w_up,
     w_down,
@@ -428,11 +512,15 @@
         pltpu.make_async_copy(src, dst, w_sem.at[n])
         for n, (src, dst) in enumerate(((w_gate, wg), (w_up, wu), (w_down, wd)))
     ]
-    for load in loads:
+    for p, (first, wide) in enumerate(CUTS):
+        loads.append(
+            pltpu.make_async_copy(
+                rows.at[:, pl.ds(first, wide)], held[p].at[0], w_sem.at[3 + 2 * p]
+            )
+        )
+        loads.append(pltpu.make_async_copy(table.at[p, 0], tables.at[p, 0], w_sem.at[4 + 2 * p]))
+    for load in loads[3:]:
         load.start()
-    for p, (first, wide) in enumerate(CUTS):
-        held[p][0] = rows[:, first : first + wide]
-        tables[p, 0] = table[p, 0]
     pl.semaphore_wait(barrier, 3 * (PLANE - 1))
 
     def remote(src, dst, out_sem, in_sem, peer):
@@ -458,6 +546,10 @@
                 copy = remote(src, dst, line_out.at[n, p, d - 1], line_in.at[n, p, d - 1], peer)
                 copy.start()
                 lines.append(copy)
+    for load in loads[:3]:
+        load.start()
+    for load in loads[3:]:
+        load.wait()
     for copy in lines:
         copy.wait_recv()
 
@@ -472,10 +564,10 @@
     def hot(p, k):
         return wide_table(p, 0) == (aim + 4.0 * k.astype(f32))[None]
 
-    def spread(way, k, src, dst):
+    def spread(way, k, src, dst, which):
         def one(n, _):
             i = n * 11 % PLANE
-            for p in range(3):
+            for p in which:
                 remote(
                     src[p].at[k, i],
                     dst[p].at[k, opposite(i)],
@@ -505,11 +597,11 @@
             ).astype(bf16)
             went[p][k] = o.reshape(PLANE, 16, wide)
             came[p][k, 0] = o[:16]
-        spread(0, k, went, came)
+            spread(0, k, went, came, (p,))
         return 0
 
     lax.fori_loop(0, ROUNDS, dispatch, 0)
-    for load in loads:
+    for load in loads[:3]:
         load.wait()
 
     def expert(k, _):
@@ -531,7 +623,7 @@
             all_of(0, k, went, came, p).wait_send()
             went[p][k] = part.reshape(PLANE, 16, wide)
             back[p][k, 0] = part[:16]
-        spread(1, k, went, back)
+        spread(1, k, went, back, (0, 1, 2))
         return 0
 
     lax.fori_loop(0, ROUNDS, expert, 0)
@@ -539,22 +631,26 @@
     for p in range(3):
         sums[p][...] = jnp.zeros_like(sums[p])
 
-    def combine(k, _):
-        for p, (first, wide) in enumerate(CUTS):
-            weights = jnp.where(hot(p, k), wide_table(p, 1), 0.0)
-            weights = weights.astype(bf16).reshape(ROUND_ROWS, 4 * ROWS)
-            all_of(1, k, went, back, p).wait_recv()
-            sums[p][...] += lax.dot_general(
-                weights,
-                back[p][k].reshape(ROUND_ROWS, wide),
-                (((0,), (0,)), ((), ())),
-                preferred_element_type=f32,
-            )
+    def combine(p, k):
+        weights = jnp.where(hot(p, k), wide_table(p, 1), 0.0)
+        weights = weights.astype(bf16).reshape(ROUND_ROWS, 4 * ROWS)
+        all_of(1, k, went, back, p).wait_recv()
+        sums[p][...] += lax.dot_general(
+            weights,
+            back[p][k].reshape(ROUND_ROWS, CUTS[p][1]),
+            (((0,), (0,)), ((), ())),
+            preferred_element_type=f32,
+        )
+
+    def add_up(k, _):
+        for p in range(3):
+            combine(p, k)
         return 0
 
-    lax.fori_loop(0, ROUNDS, combine, 0)
+    lax.fori_loop(0, ROUNDS - 1, add_up, 0)
     ends = []
     for p in range(3):
+        combine(p, jnp.int32(ROUNDS - 1))
         for d in range(1, 4):
             gave[p][d - 1] = sums[p][d * ROWS : (d + 1) * ROWS, :].astype(bf16)
             copy = remote(
@@ -571,9 +667,7 @@
         for d in range(3):
             ends[3 * p + d].wait_recv()
             total = total + got[p][d].astype(f32)
-        out[:, first : first + wide] = (
-            residual[:, first : first + wide].astype(f32) + total
-        ).astype(bf16)
+        out[:, first : first + wide] = total
     for copy in lines + ends:
         copy.wait_send()
 
@@ -585,7 +679,7 @@
     lax.fori_loop(0, ROUNDS, finish, 0)
 
 
-def experts(table, rows, residual, w_gate, w_up, w_down):
+def experts(table, rows, w_gate, w_up, w_down):
     f32, bf16 = jnp.float32, jnp.bfloat16
     vmem = pl.BlockSpec(memory_space=pltpu.VMEM)
     apart = pl.BlockSpec(memory_space=pl.ANY)
@@ -595,8 +689,8 @@
 
     return pl.pallas_call(
         expert_kernel,
-        out_shape=jax.ShapeDtypeStruct((ROWS, WIDTH), bf16),
-        in_specs=[vmem, vmem, vmem, apart, apart, apart],
+        out_shape=jax.ShapeDtypeStruct((ROWS, WIDTH), f32),
+        in_specs=[apart] * 5,
         out_specs=vmem,
         scratch_shapes=[
             pltpu.VMEM((3, 4, 2, PLANE, ROWS), bf16),
@@ -612,45 +706,16 @@
             pltpu.VMEM((WIDTH, FF), bf16),
             pltpu.VMEM((WIDTH, FF), bf16),
             pltpu.VMEM((FF, WIDTH), bf16),
-            pltpu.SemaphoreType.DMA((3,)),
+            pltpu.SemaphoreType.DMA((9,)),
             pltpu.SemaphoreType.DMA((3, 3, 3)),
             pltpu.SemaphoreType.DMA((3, 3, 3)),
             pltpu.SemaphoreType.DMA((2, ROUNDS, 3)),
             pltpu.SemaphoreType.DMA((2, ROUNDS, 3)),
         ],
         compiler_params=pltpu.CompilerParams(
-            collective_id=1, has_side_effects=True, vmem_limit_bytes=58 << 20
+            collective_id=1, has_side_effects=True, vmem_limit_bytes=60 << 20
         ),
-    )(table, rows, residual, w_gate, w_up, w_down)
-
-
-def expert_table(expert_ids, route_weights):
-    f32, bf16 = jnp.float32, jnp.bfloat16
-    chosen = expert_ids[:, :, None] == jnp.arange(DEVS)[None, None, :]
-    counts = jnp.any(chosen, axis=1)
-    before = jnp.arange(ROWS)[:, None] > jnp.arange(ROWS)[None, :]
-    rank = jnp.dot(before.astype(bf16), counts.astype(bf16), preferred_element_type=f32)
-    slots = jnp.where(counts, rank, -1.0)
-    route = jnp.sum(
-        jnp.where(chosen, (route_weights.astype(f32) / 1024.0)[:, :, None], 0.0), axis=1
-    )
-    i = jnp.arange(PLANE)
-    wanted = []
-    for p in range(3):
-        for d in range(4):
-            x, y, z, c = plane_at(p, i, *line_at(p, 4 - d, *place()))
-            context, expert = ids(x, y, z, c)
-            wanted.append(context * 8 + expert + 0 * i)
-    picks = (jnp.concatenate(wanted)[:, None] == jnp.arange(DEVS)[None, :]).astype(bf16)
-    table = jnp.stack(
-        [
-            lax.dot_general(
-                picks, v.astype(bf16), (((1,), (1,)), ((), ())), preferred_element_type=f32
-            )
-            for v in (slots, route)
-        ]
-    ).astype(bf16)
-    return table.reshape(2, 3, 4, PLANE, ROWS).transpose(1, 2, 0, 3, 4)
+    )(table, rows, w_gate, w_up, w_down)
 
 
 def shards(
@@ -673,7 +738,7 @@
     tables = [rope_tables(first * ROWS) for first in (me, DEVS - 1 - me)]
     cos = jnp.stack([jnp.concatenate([c, c], axis=1) for c, s in tables])
     sin = jnp.stack([jnp.concatenate([-s, s], axis=1) for c, s in tables])
-    residual, normed2 = before_experts(
+    residual, normed2, table = before_experts(
         tokens,
         ln1_gain.reshape(1, WIDTH),
         w_query,
@@ -685,10 +750,11 @@
         ln2_gain.reshape(1, WIDTH),
         cos,
         sin,
+        expert_ids.T,
+        route_weights.T,
     )
-
-    table = expert_table(expert_ids, route_weights)
-    return experts(table, normed2, residual, w_gate[0], w_up[0], w_down[0])
+    mixture = experts(table, normed2, w_gate[0], w_up[0], w_down[0])
+    return (residual.astype(jnp.float32) + mixture).astype(jnp.bfloat16)
 
 
 def solution(mesh):

time: 250 us -> 238 us (0.952)
  local copies, waits for them, and re-layouts: 6.72 us -> 0.01 us
  Pallas kernels: 238 us -> 233 us
    unnamed x24 -> x2, local copies, waits for them, and re-layouts: 6.53 us -> 0.01 us
    pallas_call x1, Pallas kernels: 109 us -> 105 us  [before_experts(): pl.pallas_call(layer_kernel, out_shape=(made, made, jax.ShapeDtypeStruct(...]
where the time goes in v4:
time: 238 us
  Pallas kernels  233 us (98%)
  other arithmetic  4.21 us (2%)
    pallas_call x1, Pallas kernels, experts(): pl.pallas_call(expert_kernel, out_shape=jax.ShapeDtypeStruct((ROWS, WIDTH...  129 us
    pallas_call x1, Pallas kernels, before_experts(): pl.pallas_call(layer_kernel, out_shape=(made, made, jax.ShapeDtypeStruct(...  105 us

profile of v4, /device:TPU:1, one launch (start us, length us, event | category | flops | bytes accessed | tf_op | source)
XLA Modules:
  0.0 237.7 jit_solution(2449884048207060366)
XLA Ops:
  0.0 0.5 fusion
  0.6 0.1 maximum_bitcast_fusion.2
  0.7 0.7 pad_maximum_fusion.1.sin
  1.3 0.1 maximum_bitcast_fusion
  1.4 0.7 pad_maximum_fusion.cos
  2.1 104.7 %shard_map.136 = (bf16[128,2048]{1,0:T(8,128)(2,1)}, bf16[128,2048]{1,0:T(8,128)(2,1)}, bf16[3,4,2,32,128]{4,3,2,1,0:T(8,128)(2,1)}) custom-call(bf16[128,2048]{1,0:T(8,128)(2,1)} %tokens.1, f32[1,2048]{1,0:T(1,128)} %bitcast.20, bf16[2048,256]{1,0:T(8,128)(2,1)} %far_query.1, bf16[2048,256]{1,0:T(8,128)(2,1)} %far_key.1, bf16[2048,256]{1,0:T(8,128)(2,1)} %far_value.1, ...), custom_call_target="tpu_custom_call" | custom-call | tf_op jit(solution)/shard_map/pallas_call | solution.py:386
  106.8 0.0 copy-start
  106.8 128.8 %shard_map.137 = f32[128,2048]{1,0:T(8,128)} custom-call(bf16[3,4,2,32,128]{4,3,2,1,0:T(8,128)(2,1)} %get-tuple-element.9.table, bf16[128,2048]{1,0:T(8,128)(2,1)} %get-tuple-element.10.rows, bf16[2048,768]{1,0:T(8,128)(2,1)} %bitcast.17, bf16[2048,768]{1,0:T(8,128)(2,1)} %bitcast.18, bf16[768,2048]{1,0:T(8,128)(2,1)} %bitcast.19), custom_call_target="tpu_custom_call" | custom-call | tf_op jit(solution)/shard_map/pallas_call | solution.py:690
  235.6 0.0 copy-done
  235.6 2.1 add_convert_fusion
  (3 shorter events, 0.0 us)
Async XLA Ops:
  106.8 128.8 %copy-start = (bf16[128,2048]{1,0:T(8,128)(2,1)S(1)}, bf16[128,2048]{1,0:T(8,128)(2,1)}, u32[]{:S(2)}) copy-start(bf16[128,2048]{1,0:T(8,128)(2,1)} %get-tuple-element.8) | copy-start | bytes 1572868

commit v5 on v4

--- a/solution.py
+++ b/solution.py
@@ -257,10 +257,17 @@
     acc[...] = jnp.zeros_like(acc)
     top[...] = jnp.full_like(top, -1e30)
 
-    def step(p, block, jz, jy, high_half, base, masked):
-        part = pl.ds(2 * high_half, 2)
-        k = buf[0, jz, jy, :, part].reshape(CHUNK, HEAD)
-        v = buf[1, jz, jy, :, part].reshape(CHUNK, HEAD)
+    def step(p, block, places, base, masked):
+        k, v = (
+            jnp.concatenate(
+                [
+                    buf[n, jz, jy, :, pl.ds(2 * high_half, 2)].reshape(CHUNK, HEAD)
+                    for jz, jy, high_half in places
+                ],
+                axis=0,
+            )
+            for n in range(2)
+        )
         ke = jnp.concatenate([k, k], axis=1)
         ve = jnp.concatenate([v, jnp.ones_like(v)], axis=1)
         scores = [
@@ -290,21 +297,36 @@
     def chunks(first_chunk, last_chunk, find):
         def body(n, _):
             p = n % 2
-            jz, jy, high_half = find(n // 2)
             block = b + p * (DEVS - 1 - 2 * b)
-            base = (jz * 2 + jy) * 16 + high_half * 4
-
-            @pl.when(base + 11 < block)
+            places = [find(n // 2 * 2), find(n // 2 * 2 + 1)]
+            bases = [(jz * 2 + jy) * 16 + high_half * 4 for jz, jy, high_half in places]
+            whole = (bases[0] + 11 < block) & (bases[1] + 11 < block)
+
+            @pl.when(whole)
             def _():
-                step(p, block, jz, jy, high_half, base, False)
-
-            @pl.when((base <= block) & (base + 11 >= block))
+                step(p, block, places, 0, False)
+
+            def one(m, _):
+                place_m = find(n // 2 * 2 + m)
+                base = (place_m[0] * 2 + place_m[1]) * 16 + place_m[2] * 4
+
+                @pl.when(base + 11 < block)
+                def _():
+                    step(p, block, [place_m], base, False)
+
+                @pl.when((base <= block) & (base + 11 >= block))
+                def _():
+                    step(p, block, [place_m], base, True)
+
+                return 0
+
+            @pl.when(jnp.logical_not(whole))
             def _():
-                step(p, block, jz, jy, high_half, base, True)
+                lax.fori_loop(0, 2, one, 0)
 
             return 0
 
-        lax.fori_loop(2 * first_chunk, 2 * last_chunk, body, 0)
+        lax.fori_loop(first_chunk, last_chunk, body, 0)
 
     def early(m):
         late = m // 6
@@ -317,7 +339,7 @@
 
     for copy in handed[:6]:
         copy.wait_recv()
-    chunks(0, 5, early)
+    chunks(0, 4, early)
     fourth[0].wait_recv()
     far = lax.rem(z + 2, 4)
     handed.append(send(of_z(far, pl.ds(0, 1)), of_z(far, pl.ds(0, 1)), other))
@@ -331,7 +353,7 @@
     o1.wait_recv()
     o3 = send(wo.at[0, c], wo.at[2, c], along)
     handed_o = [send(wo.at[0, c], wo.at[0, c], other)]
-    chunks(5, 10, early)
+    chunks(4, 10, early)
     o2.wait_recv()
     handed_o.append(send(wo.at[1, c], wo.at[1, c], other))
     for copy in handed[6:]:

time: 238 us -> 243 us (1.021); the launches traced: 238 us -> 240 us
  no operation moved by 1% of the time
where the time goes in v5:
time: 243 us; the launch traced here: 240 us
  Pallas kernels  235 us (97%)
  other arithmetic  4.21 us (2%)
    pallas_call x1, Pallas kernels, experts(): pl.pallas_call(expert_kernel, out_shape=jax.ShapeDtypeStruct((ROWS, WIDTH...  129 us
    pallas_call x1, Pallas kernels, before_experts(): pl.pallas_call(layer_kernel, out_shape=(made, made, jax.ShapeDtypeStruct(...  106 us

profile of v5, /device:TPU:1, one launch (start us, length us, event | category | flops | bytes accessed | tf_op | source)
XLA Modules:
  0.0 239.7 jit_solution(15062818548481838669)
XLA Ops:
  0.0 0.5 fusion
  0.6 0.1 maximum_bitcast_fusion.2
  0.7 0.7 pad_maximum_fusion.1.sin
  1.3 0.1 maximum_bitcast_fusion
  1.4 0.7 pad_maximum_fusion.cos
  2.1 105.8 %shard_map.136 = (bf16[128,2048]{1,0:T(8,128)(2,1)}, bf16[128,2048]{1,0:T(8,128)(2,1)}, bf16[3,4,2,32,128]{4,3,2,1,0:T(8,128)(2,1)}) custom-call(bf16[128,2048]{1,0:T(8,128)(2,1)} %tokens.1, f32[1,2048]{1,0:T(1,128)} %bitcast.20, bf16[2048,256]{1,0:T(8,128)(2,1)} %far_query.1, bf16[2048,256]{1,0:T(8,128)(2,1)} %far_key.1, bf16[2048,256]{1,0:T(8,128)(2,1)} %far_value.1, ...), custom_call_target="tpu_custom_call" | custom-call | tf_op jit(solution)/shard_map/pallas_call | solution.py:408
  107.9 0.0 copy-start
  107.9 129.2 %shard_map.137 = f32[128,2048]{1,0:T(8,128)} custom-call(bf16[3,4,2,32,128]{4,3,2,1,0:T(8,128)(2,1)} %get-tuple-element.9.table, bf16[128,2048]{1,0:T(8,128)(2,1)} %get-tuple-element.10.rows, bf16[2048,768]{1,0:T(8,128)(2,1)} %bitcast.17, bf16[2048,768]{1,0:T(8,128)(2,1)} %bitcast.18, bf16[768,2048]{1,0:T(8,128)(2,1)} %bitcast.19), custom_call_target="tpu_custom_call" | custom-call | tf_op jit(solution)/shard_map/pallas_call | solution.py:712
  237.1 0.0 copy-done
  237.1 2.1 add_convert_fusion
  (3 shorter events, 0.0 us)
Async XLA Ops:
  107.9 129.2 %copy-start = (bf16[128,2048]{1,0:T(8,128)(2,1)S(1)}, bf16[128,2048]{1,0:T(8,128)(2,1)}, u32[]{:S(2)}) copy-start(bf16[128,2048]{1,0:T(8,128)(2,1)} %get-tuple-element.8) | copy-start | bytes 1572868
